TPU v7x, 512 devices: a whole 4x4x16 slice. The times are simulated.
512 devices in a mesh: ctx: 64 (over y_lo, z, core), head: 8 (over x, y_hi).
Axes of the slice: x: 4, y: 4 (y_hi: 2, y_lo: 2; y = y_hi * 2 + y_lo), z: 16, core: 2. Of those that a mesh axis runs over, the one named last changes fastest.
Arguments:
- queries: bfloat16 [16384, 8192], P(('ctx', 'head')), may hold values from -6 to 6
- keys: bfloat16 [16384, 1024], P(('ctx', 'head')), may hold values from -6 to 6
- values: bfloat16 [16384, 1024], P(('ctx', 'head')), may hold values from -6 to 6
- output_gradient: bfloat16 [16384, 8192], P(('ctx', 'head')), may hold values from -6 to 6
- doc_lengths: int32 [32], replicated, may hold values from 1 to 1024, 16384 in all
Outputs:
- attention: bfloat16 [16384, 8192], P(('ctx', 'head'))
- grad_queries: bfloat16 [16384, 8192], P(('ctx', 'head'))
- key_gradient: bfloat16 [16384, 1024], P(('ctx', 'head'))
- value_gradient: bfloat16 [16384, 1024], P(('ctx', 'head'))
Inputs may be any that keep to these rules, and one draw needn't show every extreme that they name: `doc_lengths`: document lengths sum to 16384; the longest has exactly 1024 tokens.
All inputs are finite; a program needn't handle non-finite values.
Results may differ from a plain program's by a relative error of at most 0.03.
Values may be sent and summed in bfloat16 or wider, within the bound.
A program may use at most 64 MiB of HBM per device.

v0:
```python
import math

import jax
import jax.numpy as jnp
from jax import lax
from jax.sharding import PartitionSpec as P

HEAD_WIDTH = 128
QUERY_HEADS = 64
KEY_VALUE_HEADS = 8
SPAN = 4


def shifted(block, axis, distance):
    devices = range(lax.axis_size(axis))
    route = [(i - distance, i) for i in devices if i - distance in devices]
    return lax.ppermute(block, axis, route)


def document_ids(doc_ends, start, count):
    positions = start + lax.iota(jnp.int32, count)
    ids = jnp.sum((doc_ends[None, :] <= positions[:, None]).astype(jnp.int32), axis=1)
    return (ids, positions)


def to_columns(block_size):
    return block_size.reshape(block_size.shape[0], 1, -1)


def shards(queries, keys, values, output_gradient, doc_lengths):
    head_groups = lax.axis_size("head")
    incoming_rows = queries.shape[0]
    heads_local = QUERY_HEADS // head_groups
    local_key_value = KEY_VALUE_HEADS // head_groups
    heads_per_group = QUERY_HEADS // KEY_VALUE_HEADS
    score_scale = 1.0 / math.sqrt(HEAD_WIDTH)
    query_in, key_in, value_in, grad_in = (
        lax.all_to_all(
            queries.reshape(incoming_rows, head_groups, heads_local * HEAD_WIDTH),
            "head",
            split_axis=1,
            concat_axis=0,
            tiled=True,
        ),
        lax.all_to_all(
            keys.reshape(incoming_rows, head_groups, local_key_value * HEAD_WIDTH),
            "head",
            split_axis=1,
            concat_axis=0,
            tiled=True,
        ),
        lax.all_to_all(
            values.reshape(incoming_rows, head_groups, local_key_value * HEAD_WIDTH),
            "head",
            split_axis=1,
            concat_axis=0,
            tiled=True,
        ),
        lax.all_to_all(
            output_gradient.reshape(incoming_rows, head_groups, heads_local * HEAD_WIDTH),
            "head",
            split_axis=1,
            concat_axis=0,
            tiled=True,
        ),
    )
    shard_rows = query_in.shape[0]
    query_local = query_in.reshape(shard_rows, local_key_value, heads_per_group, HEAD_WIDTH)
    grad_local = grad_in.reshape(shard_rows, local_key_value, heads_per_group, HEAD_WIDTH)
    doc_ends = jnp.cumsum(doc_lengths)
    own_index = lax.axis_index("ctx")
    own_start = own_index * shard_rows
    key_blocks = [key_in]
    value_blocks = [value_in]
    for distance in range(1, SPAN + 1):
        earlier_key, earlier_value = shifted((key_in, value_in), "ctx", distance)
        key_blocks.append(earlier_key)
        value_blocks.append(earlier_value)
    rows_part = query_local.shape[0]
    query_ids, query_pos = document_ids(doc_ends, own_start, rows_part)
    allowed_sets = []
    for attend_distance in range(SPAN + 1):
        key_ids, key_pos = document_ids(
            doc_ends, own_start - attend_distance * shard_rows, shard_rows
        )
        allowed_sets.append(
            (query_ids[:, None] == key_ids[None, :])
            & (key_pos[None, :] >= 0)
            & (key_pos[None, :] <= query_pos[:, None])
        )

    def score_block(key_block, allowed):
        raw = (
            jnp.einsum("sagd,tad->agst", query_local, key_block, preferred_element_type=jnp.float32)
            * score_scale
        )
        return jnp.where(allowed, raw, -jnp.inf)

    first = score_block(key_blocks[0], allowed_sets[0])
    row_max = jnp.max(first, axis=-1)
    row_total = jnp.sum(jnp.exp(first - row_max[..., None]), axis=-1)
    for attend_distance in range(1, SPAN + 1):
        old_max = row_max
        old_total = row_total
        merge_key_block = key_blocks[attend_distance]
        merge_allowed = allowed_sets[attend_distance]
        scores = score_block(merge_key_block, merge_allowed)
        new_max = jnp.maximum(old_max, jnp.max(scores, axis=-1))
        new_total = old_total * jnp.exp(old_max - new_max) + jnp.sum(
            jnp.exp(scores - new_max[..., None]), axis=-1
        )
        row_max = new_max
        row_total = new_total
    log_total = row_max + jnp.log(row_total)

    def prob_block(key_block, allowed):
        return jnp.exp(score_block(key_block, allowed) - log_total[..., None])

    zero_out = jnp.zeros((rows_part, local_key_value, heads_per_group, HEAD_WIDTH), jnp.float32)
    out_sum = zero_out
    for attend_distance in range(SPAN + 1):
        out_key_block = key_blocks[attend_distance]
        out_value_block = value_blocks[attend_distance]
        out_allowed = allowed_sets[attend_distance]
        weights = prob_block(out_key_block, out_allowed).astype(jnp.bfloat16)
        out_sum = out_sum + jnp.einsum(
            "agst,tad->sagd", weights, out_value_block, preferred_element_type=jnp.float32
        )
    attention_part = out_sum.astype(jnp.bfloat16)
    delta = jnp.transpose(
        jnp.sum(grad_local.astype(jnp.float32) * attention_part.astype(jnp.float32), axis=-1),
        (1, 2, 0),
    )
    query_grad = zero_out
    key_terms = []
    value_terms = []
    for attend_distance in range(SPAN + 1):
        grad_key_block = key_blocks[attend_distance]
        value_block = value_blocks[attend_distance]
        grad_allowed = allowed_sets[attend_distance]
        probs = prob_block(grad_key_block, grad_allowed)
        prob_grad = jnp.einsum(
            "sagd,tad->agst", grad_local, value_block, preferred_element_type=jnp.float32
        )
        dscore = (probs * (prob_grad - delta[..., None]) * score_scale).astype(jnp.bfloat16)
        query_term = jnp.einsum(
            "agst,tad->sagd", dscore, grad_key_block, preferred_element_type=jnp.float32
        )
        key_term = jnp.einsum(
            "agst,sagd->tad", dscore, query_local, preferred_element_type=jnp.float32
        )
        value_term = jnp.einsum(
            "agst,sagd->tad",
            probs.astype(jnp.bfloat16),
            grad_local,
            preferred_element_type=jnp.float32,
        )
        query_term, key_term, value_term = (query_term, key_term, value_term)
        query_grad = query_grad + query_term
        key_terms.append(key_term)
        value_terms.append(value_term)
    query_grad_b = query_grad.astype(jnp.bfloat16)
    key_stack = jnp.stack(key_terms)
    value_stack = jnp.stack(value_terms)
    attention_out = lax.all_to_all(
        to_columns(attention_part), "head", split_axis=0, concat_axis=1, tiled=True
    ).reshape(incoming_rows, QUERY_HEADS * HEAD_WIDTH)
    key_total = key_stack[0]
    value_total = value_stack[0]
    for distance in range(1, SPAN + 1):
        back_key, back_value = shifted(
            (key_stack[distance], value_stack[distance]), "ctx", -distance
        )
        key_total = key_total + back_key
        value_total = value_total + back_value
    piece_list = (
        lax.all_to_all(to_columns(query_grad_b), "head", split_axis=0, concat_axis=1, tiled=True),
        lax.all_to_all(
            to_columns(key_total.astype(jnp.bfloat16)),
            "head",
            split_axis=0,
            concat_axis=1,
            tiled=True,
        ),
        lax.all_to_all(
            to_columns(value_total.astype(jnp.bfloat16)),
            "head",
            split_axis=0,
            concat_axis=1,
            tiled=True,
        ),
    )
    return (
        attention_out,
        piece_list[0].reshape(incoming_rows, QUERY_HEADS * HEAD_WIDTH),
        piece_list[1].reshape(incoming_rows, KEY_VALUE_HEADS * HEAD_WIDTH),
        piece_list[2].reshape(incoming_rows, KEY_VALUE_HEADS * HEAD_WIDTH),
    )


def solution(mesh):
    placed = (
        P(("ctx", "head"), None),
        P(("ctx", "head"), None),
        P(("ctx", "head"), None),
        P(("ctx", "head"), None),
        P(),
    )
    return jax.shard_map(
        shards,
        mesh=mesh,
        in_specs=placed,
        out_specs=(
            P(("ctx", "head"), None),
            P(("ctx", "head"), None),
            P(("ctx", "head"), None),
            P(("ctx", "head"), None),
        ),
        check_vma=False,
    )
```

profile of v0, /device:TPU:8, one launch (start us, length us, event | category | flops | bytes accessed | tf_op | source)
XLA Modules:
  0.0 210.4 jit_solution(6415859986649255586)
XLA Ops:
  2.1 6.0 %all-to-all-start = ((bf16[32,8,128]{2,0,1:T(8,128)(2,1)}), bf16[32,8,128]{2,0,1:T(8,128)(2,1)S(1)}, u32[]{:S(2)}, u32[]{:S(2)}) async-start(bf16[32,8,128]{2,0,1:T(8,128)(2,1)} %copy_bitcast_fusion.6), calls=%async_computation | async-start | bytes 131072 | tf_op jit(solution)/shard_map/all_to_all | solution.py:45
  9.1 1.5 copy_bitcast_fusion.5
  10.6 1.9 copy.495
  12.4 1.9 copy.494
  14.3 1.6 all-to-all-done
  15.9 5.6 %all-to-all-start.2 = ((bf16[32,8,128]{2,0,1:T(8,128)(2,1)}), bf16[32,8,128]{2,0,1:T(8,128)(2,1)S(1)}, u32[]{:S(2)}, u32[]{:S(2)}) async-start(bf16[32,8,128]{2,0,1:T(8,128)(2,1)} %copy_bitcast_fusion.5), calls=%async_computation.2 | async-start | bytes 131072 | tf_op jit(solution)/shard_map/all_to_all | solution.py:52
  21.5 7.8 %all-to-all-done.2 = bf16[32,8,128]{2,0,1:T(8,128)(2,1)S(1)} async-done(((bf16[32,8,128]{2,0,1:T(8,128)(2,1)}), bf16[32,8,128]{2,0,1:T(8,128)(2,1)S(1)}, u32[]{:S(2)}, u32[]{:S(2)}) %all-to-all-start.2) | async-done | bytes 65568 | tf_op jit(solution)/shard_map/all_to_all | solution.py:52
  29.3 3.5 %all-to-all-start.1 = ((bf16[32,8,1024]{2,0,1:T(8,128)(2,1)}), bf16[32,8,1024]{2,0,1:T(8,128)(2,1)S(1)}, u32[]{:S(2)}, u32[]{:S(2)}) async-start(bf16[32,8,1024]{2,0,1:T(8,128)(2,1)} %bitcast.412), calls=%async_computation.1 | async-start | bytes 1048576 | tf_op jit(solution)/shard_map/all_to_all | solution.py:38
  32.9 1.4 compare_and_fusion.3
  35.0 5.2 %collective-permute-start.7 = (bf16[256,1,128]{0,2,1:T(8,128)(2,1)}, bf16[256,1,128]{0,2,1:T(8,128)(2,1)}, u32[]{:S(2)}, u32[]{:S(2)}) collective-permute-start(bf16[256,1,128]{0,2,1:T(8,128)(2,1)} %copy.339), channel_id=1, source_target_pairs={{0,32},{8,40},{16,48},{24,56},{32,64},{40,72},{48,80},{56,88},{64,... | collective-permute-start | bytes 196616 | tf_op jit(solution)/shard_map/ppermute | solution.py:17
  40.2 1.9 collective-permute-start.6
  42.1 4.1 %collective-permute-start.5 = (bf16[256,1,128]{0,2,1:T(8,128)(2,1)}, bf16[256,1,128]{0,2,1:T(8,128)(2,1)S(1)}, u32[]{:S(2)}, u32[]{:S(2)}) collective-permute-start(bf16[256,1,128]{0,2,1:T(8,128)(2,1)} %copy.339), channel_id=1, source_target_pairs={{0,16},{8,24},{16,32},{24,40},{32,48},{40,56},{48,64},{56,72},{64,... | collective-permute-start | bytes 196616 | tf_op jit(solution)/shard_map/ppermute | solution.py:17
  46.2 5.9 %collective-permute-start.4 = (bf16[256,1,128]{0,2,1:T(8,128)(2,1)}, bf16[256,1,128]{0,2,1:T(8,128)(2,1)S(1)}, u32[]{:S(2)}, u32[]{:S(2)}) collective-permute-start(bf16[256,1,128]{0,2,1:T(8,128)(2,1)} %copy.339), channel_id=1, source_target_pairs={{0,8},{8,16},{16,24},{24,32},{32,40},{40,48},{48,56},{56,64},{64,7... | collective-permute-start | bytes 196616 | tf_op jit(solution)/shard_map/ppermute | solution.py:17
  52.2 1.9 collective-permute-start
  54.1 7.1 %all-to-all-start.4 = ((bf16[32,8,1024]{2,0,1:T(8,128)(2,1)}), bf16[32,8,1024]{2,0,1:T(8,128)(2,1)S(1)}, u32[]{:S(2)}, u32[]{:S(2)}) async-start(bf16[32,8,1024]{2,0,1:T(8,128)(2,1)} %bitcast.411), calls=%async_computation.4 | async-start | bytes 1048576 | tf_op jit(solution)/shard_map/all_to_all | solution.py:59
  61.9 3.8 %collective-permute-start.1 = (bf16[256,1,128]{2,0,1:T(8,128)(2,1)S(1)}, bf16[256,1,128]{2,0,1:T(8,128)(2,1)S(1)}, u32[]{:S(2)}, u32[]{:S(2)}) collective-permute-start(bf16[256,1,128]{2,0,1:T(8,128)(2,1)S(1)} %bitcast.447), channel_id=1, source_target_pairs={{0,16},{8,24},{16,32},{24,40},{32,48},{40,56},{48,64},{56,72},{64,... | collective-permute-start | bytes 196616 | tf_op jit(solution)/shard_map/ppermute | solution.py:17
  65.7 2.6 %fusion.103 = (f32[8,256]{1,0:T(8,128)S(1)}, f32[1,8,256,256]{2,3,1,0:T(8,128)}) fusion(bf16[256,8,128]{2,1,0:T(8,128)(2,1)S(1)} %bitcast.426, bf16[256,1,128]{2,0,1:T(8,128)(2,1)} %collective-permute-done, pred[256,256]{0,1:T(8,128)(4,1)S(1)} %copy-done.19), kind=kOutput, calls=%fused_computation.156 | convolution fusion | flops 135788544 | bytes 2760704 | tf_op jit(solution)/shard_map/sagd,tad->agst/dot_general | solution.py:94
  68.3 1.8 collective-permute-done.1
  70.1 4.3 %collective-permute-start.2 = (bf16[256,1,128]{2,0,1:T(8,128)(2,1)S(1)}, bf16[256,1,128]{2,0,1:T(8,128)(2,1)}, u32[]{:S(2)}, u32[]{:S(2)}) collective-permute-start(bf16[256,1,128]{2,0,1:T(8,128)(2,1)S(1)} %bitcast.448), channel_id=1, source_target_pairs={{0,24},{8,32},{16,40},{24,48},{32,56},{40,64},{48,72},{56,80},{64,... | collective-permute-start | bytes 196616 | tf_op jit(solution)/shard_map/ppermute | solution.py:17
  74.4 2.4 %fusion.101 = (f32[8,256]{1,0:T(8,128)}, f32[1,8,256,256]{2,3,1,0:T(8,128)}) fusion(bf16[256,8,128]{2,1,0:T(8,128)(2,1)S(1)} %bitcast.427, bf16[256,1,128]{2,0,1:T(8,128)(2,1)S(1)} %collective-permute-done.1, pred[256,256]{0,1:T(8,128)(4,1)S(1)} %copy-done.18), kind=kOutput, calls=%fused_computation.154 | convolution fusion | flops 135788544 | bytes 2760704 | tf_op jit(solution)/shard_map/sagd,tad->agst/dot_general | solution.py:94
  77.2 1.7 collective-permute-done.2
  78.9 2.8 %collective-permute-start.3 = (bf16[256,1,128]{2,0,1:T(8,128)(2,1)S(1)}, bf16[256,1,128]{2,0,1:T(8,128)(2,1)S(1)}, u32[]{:S(2)}, u32[]{:S(2)}) collective-permute-start(bf16[256,1,128]{2,0,1:T(8,128)(2,1)S(1)} %bitcast.449), channel_id=1, source_target_pairs={{0,32},{8,40},{16,48},{24,56},{32,64},{40,72},{48,80},{56,88},{64,... | collective-permute-start | bytes 196616 | tf_op jit(solution)/shard_map/ppermute | solution.py:17
  81.7 1.3 fusion.100
  83.8 4.9 %collective-permute-done.3 = bf16[256,1,128]{2,0,1:T(8,128)(2,1)S(1)} collective-permute-done((bf16[256,1,128]{2,0,1:T(8,128)(2,1)S(1)}, bf16[256,1,128]{2,0,1:T(8,128)(2,1)S(1)}, u32[]{:S(2)}, u32[]{:S(2)}) %collective-permute-start.3) | collective-permute-done | bytes 65568 | tf_op jit(solution)/shard_map/ppermute | solution.py:17
  89.8 1.7 copy-done.3
  92.5 1.1 convolution_bitcast_fusion
  93.6 1.1 convolution_bitcast_fusion.1
  94.8 1.1 convolution_bitcast_fusion.2
  96.4 1.1 convolution_bitcast_fusion.3
  97.5 1.9 collective-permute-start.12
  99.5 1.9 collective-permute-start.13
  101.4 1.6 convolution_add_fusion.1
  103.0 2.3 %collective-permute-start.14 = (f32[256,1,128]{2,0,1:T(8,128)}, f32[256,1,128]{2,0,1:T(8,128)}, u32[]{:S(2)}, u32[]{:S(2)}) collective-permute-start(f32[256,1,128]{2,0,1:T(8,128)} %convolution_bitcast_fusion.1), channel_id=1, source_target_pairs={{24,0},{32,8},{40,16},{48,24},{56,32},{64,40},{72,48},{80,56},{88,... | collective-permute-start | bytes 393224 | tf_op jit(solution)/shard_map/ppermute | solution.py:17
  105.3 2.3 %fusion.54 = f32[8,256,128]{1,2,0:T(8,128)} fusion(f32[1,8,256,256]{2,3,1,0:T(8,128)S(1)} %get-tuple-element.23, f32[8,256]{1,0:T(8,128)S(1)} %log_add_fusion, bf16[256,1,128]{0,2,1:T(8,128)(2,1)} %collective-permute-done.6), kind=kOutput, calls=%fused_computation.85 | convolution fusion | flops 135266304 | bytes 3219456 | tf_op jit(solution)/shard_map/agst,tad->sagd/dot_general | solution.py:126
  107.6 4.6 %collective-permute-start.15 = (f32[256,1,128]{2,0,1:T(8,128)}, f32[256,1,128]{2,0,1:T(8,128)}, u32[]{:S(2)}, u32[]{:S(2)}) collective-permute-start(f32[256,1,128]{2,0,1:T(8,128)} %convolution_bitcast_fusion), channel_id=1, source_target_pairs={{32,0},{40,8},{48,16},{56,24},{64,32},{72,40},{80,48},{88,56},{96,... | collective-permute-start | bytes 393224 | tf_op jit(solution)/shard_map/ppermute | solution.py:17
  112.3 2.3 %fusion.57 = f32[8,256,128]{1,2,0:T(8,128)} fusion(f32[1,8,256,256]{2,3,1,0:T(8,128)S(1)} %get-tuple-element.21, f32[8,256]{1,0:T(8,128)S(1)} %log_add_fusion, bf16[256,1,128]{0,2,1:T(8,128)(2,1)} %collective-permute-done.7), kind=kOutput, calls=%fused_computation.86 | convolution fusion | flops 135266304 | bytes 3219456 | tf_op jit(solution)/shard_map/agst,tad->sagd/dot_general | solution.py:126
  114.6 2.1 %copy.353 = f32[8,32,1,1024]{3,2,1,0:T(1,128)} copy(f32[8,32,1,1024]{3,0,1,2:T(8,128)S(1)} %get-tuple-element.14) | data formatting | bytes 2097152 | tf_op jit(solution)/shard_map/convert_element_type | solution.py:131
  116.7 2.5 %copy.354 = f32[256,1,8,128]{0,3,2,1:T(8,128)} copy(f32[256,1,8,128]{3,2,1,0:T(8,128)} %bitcast.435) | data formatting | bytes 2097152 | tf_op jit(solution)/shard_map/convert_element_type | solution.py:131
  119.2 4.2 %multiply_reduce_fusion = (f32[256,8]{0,1:T(8,128)S(1)}, bf16[8,256,128]{1,2,0:T(8,128)(2,1)}) fusion(f32[256,1,8,128]{0,3,2,1:T(8,128)} %copy.354, f32[8,256,128]{1,2,0:T(8,128)} %fusion.57, f32[8,256,128]{1,2,0:T(8,128)} %fusion.54, f32[8,256,128]{1,2,0:T(8,128)} %convolution_add_fusion.1, f32[1,8,256,256]{2,3,1,0:T(8,128)} %get-tuple-element.25, ...), kind=kOutput, calls=%fused_computation.80 | convolution fusion | flops 137099264 | bytes 6897664 | tf_op jit(solution)/shard_map/agst,tad->sagd/dot_general | solution.py:126
  125.0 1.7 fusion.24
  126.7 1.1 convolution_bitcast_fusion.5
  127.8 1.6 fusion.23
  131.2 1.1 convolution_bitcast_fusion.8
  132.2 1.9 collective-permute-start.8
  135.4 1.3 fusion.67
  136.7 2.2 %fusion.70 = f32[8,256,128]{1,2,0:T(8,128)} fusion(bf16[8,256,256]{1,2,0:T(8,128)(2,1)S(1)} %fusion.23, bf16[256,1,128]{2,0,1:T(8,128)(2,1)} %collective-permute-done.2), kind=kOutput, calls=%fused_computation.107 | convolution fusion | flops 134217728 | bytes 2162688 | tf_op jit(solution)/shard_map/agst,tad->sagd/dot_general | solution.py:146
  139.0 2.2 %convolution_add_fusion.3 = f32[8,256,128]{1,2,0:T(8,128)} fusion(f32[8,256,128]{1,2,0:T(8,128)S(1)} %fusion.104, bf16[8,256,256]{1,2,0:T(8,128)(2,1)S(1)} %fusion.21, bf16[256,1,128]{2,0,1:T(8,128)(2,1)} %collective-permute-done), kind=kOutput, calls=%fused_computation.50 | convolution fusion | flops 134479872 | bytes 3211264 | tf_op jit(solution)/shard_map/agst,tad->sagd/dot_general | solution.py:146
  141.1 1.1 convolution_bitcast_fusion.7
  142.2 3.2 %collective-permute-start.9 = (f32[256,1,128]{2,0,1:T(8,128)}, f32[256,1,128]{2,0,1:T(8,128)S(1)}, u32[]{:S(2)}, u32[]{:S(2)}) collective-permute-start(f32[256,1,128]{2,0,1:T(8,128)} %convolution_bitcast_fusion.7), channel_id=1, source_target_pairs={{16,0},{24,8},{32,16},{40,24},{48,32},{56,40},{64,48},{72,56},{80,... | collective-permute-start | bytes 393224 | tf_op jit(solution)/shard_map/ppermute | solution.py:17
  145.5 5.7 %collective-permute-start.10 = (f32[256,1,128]{2,0,1:T(8,128)}, f32[256,1,128]{2,0,1:T(8,128)}, u32[]{:S(2)}, u32[]{:S(2)}) collective-permute-start(f32[256,1,128]{2,0,1:T(8,128)} %convolution_bitcast_fusion.6), channel_id=1, source_target_pairs={{24,0},{32,8},{40,16},{48,24},{56,32},{64,40},{72,48},{80,56},{88,... | collective-permute-start | bytes 393224 | tf_op jit(solution)/shard_map/ppermute | solution.py:17
  151.2 2.5 %collective-permute-start.11 = (f32[256,1,128]{2,0,1:T(8,128)}, f32[256,1,128]{2,0,1:T(8,128)}, u32[]{:S(2)}, u32[]{:S(2)}) collective-permute-start(f32[256,1,128]{2,0,1:T(8,128)} %convolution_bitcast_fusion.5), channel_id=1, source_target_pairs={{32,0},{40,8},{48,16},{56,24},{64,32},{72,40},{80,48},{88,56},{96,... | collective-permute-start | bytes 393224 | tf_op jit(solution)/shard_map/ppermute | solution.py:17
  153.7 1.6 fusion.40
  157.2 6.3 %all-to-all-start.7 = ((bf16[8,2,2048]{2,1,0:T(2,128)(2,1)}), bf16[8,2,2048]{2,1,0:T(2,128)(2,1)S(1)}, u32[]{:S(2)}, u32[]{:S(2)}) async-start(bf16[8,2,2048]{2,1,0:T(2,128)(2,1)} %reshape.555), calls=%async_computation.7 | async-start | bytes 131072 | tf_op jit(solution)/shard_map/all_to_all | solution.py:185
  163.5 1.8 fusion.39
  166.5 4.7 %all-to-all-done.7 = bf16[8,2,2048]{2,1,0:T(2,128)(2,1)S(1)} async-done(((bf16[8,2,2048]{2,1,0:T(2,128)(2,1)}), bf16[8,2,2048]{2,1,0:T(2,128)(2,1)S(1)}, u32[]{:S(2)}, u32[]{:S(2)}) %all-to-all-start.7) | async-done | bytes 65568 | tf_op jit(solution)/shard_map/all_to_all | solution.py:185
  171.2 3.4 %all-to-all-start.6 = ((bf16[8,2,2048]{2,1,0:T(2,128)(2,1)}), bf16[8,2,2048]{2,1,0:T(2,128)(2,1)S(1)}, u32[]{:S(2)}, u32[]{:S(2)}) async-start(bf16[8,2,2048]{2,1,0:T(2,128)(2,1)} %reshape.553), calls=%async_computation.6 | async-start | bytes 131072 | tf_op jit(solution)/shard_map/all_to_all | solution.py:178
  174.6 2.0 fusion.30
  177.8 1.2 reshape.551
  179.0 3.3 %all-to-all-done.6 = bf16[8,2,2048]{2,1,0:T(2,128)(2,1)S(1)} async-done(((bf16[8,2,2048]{2,1,0:T(2,128)(2,1)}), bf16[8,2,2048]{2,1,0:T(2,128)(2,1)S(1)}, u32[]{:S(2)}, u32[]{:S(2)}) %all-to-all-start.6) | async-done | bytes 65568 | tf_op jit(solution)/shard_map/all_to_all | solution.py:178
  182.3 3.8 %all-to-all-start.5 = ((bf16[8,2,16384]{2,1,0:T(2,128)(2,1)}), bf16[8,2,16384]{2,1,0:T(2,128)(2,1)S(1)}, u32[]{:S(2)}, u32[]{:S(2)}) async-start(bf16[8,2,16384]{2,1,0:T(2,128)(2,1)} %reshape.551), calls=%async_computation.5 | async-start | bytes 1048576 | tf_op jit(solution)/shard_map/all_to_all | solution.py:177
  187.2 1.2 reshape.549
  188.4 7.4 %all-to-all-done.5 = bf16[8,2,16384]{2,1,0:T(2,128)(2,1)S(1)} async-done(((bf16[8,2,16384]{2,1,0:T(2,128)(2,1)}), bf16[8,2,16384]{2,1,0:T(2,128)(2,1)S(1)}, u32[]{:S(2)}, u32[]{:S(2)}) %all-to-all-start.5) | async-done | bytes 524320 | tf_op jit(solution)/shard_map/all_to_all | solution.py:177
  195.8 3.5 %all-to-all-start.3 = ((bf16[8,2,16384]{2,1,0:T(2,128)(2,1)}), bf16[8,2,16384]{2,1,0:T(2,128)(2,1)S(1)}, u32[]{:S(2)}, u32[]{:S(2)}) async-start(bf16[8,2,16384]{2,1,0:T(2,128)(2,1)} %reshape.549), calls=%async_computation.3 | async-start | bytes 1048576 | tf_op jit(solution)/shard_map/all_to_all | solution.py:165
  202.3 6.5 %all-to-all-done.3 = bf16[8,2,16384]{2,1,0:T(2,128)(2,1)S(1)} async-done(((bf16[8,2,16384]{2,1,0:T(2,128)(2,1)}), bf16[8,2,16384]{2,1,0:T(2,128)(2,1)S(1)}, u32[]{:S(2)}, u32[]{:S(2)}) %all-to-all-start.3) | async-done | bytes 524320 | tf_op jit(solution)/shard_map/all_to_all | solution.py:165
  (110 shorter events, 21.9 us)
Async XLA Ops:
  0.6 0.8 copy-start
  2.1 13.8 %all-to-all-start = ((bf16[32,8,128]{2,0,1:T(8,128)(2,1)}), bf16[32,8,128]{2,0,1:T(8,128)(2,1)S(1)}, u32[]{:S(2)}, u32[]{:S(2)}) async-start(bf16[32,8,128]{2,0,1:T(8,128)(2,1)} %copy_bitcast_fusion.6), calls=%async_computation | async-start | bytes 131072 | tf_op jit(solution)/shard_map/all_to_all | solution.py:45
  15.9 13.4 %all-to-all-start.2 = ((bf16[32,8,128]{2,0,1:T(8,128)(2,1)}), bf16[32,8,128]{2,0,1:T(8,128)(2,1)S(1)}, u32[]{:S(2)}, u32[]{:S(2)}) async-start(bf16[32,8,128]{2,0,1:T(8,128)(2,1)} %copy_bitcast_fusion.5), calls=%async_computation.2 | async-start | bytes 131072 | tf_op jit(solution)/shard_map/all_to_all | solution.py:52
  29.3 24.8 %all-to-all-start.1 = ((bf16[32,8,1024]{2,0,1:T(8,128)(2,1)}), bf16[32,8,1024]{2,0,1:T(8,128)(2,1)S(1)}, u32[]{:S(2)}, u32[]{:S(2)}) async-start(bf16[32,8,1024]{2,0,1:T(8,128)(2,1)} %bitcast.412), calls=%async_computation.1 | async-start | bytes 1048576 | tf_op jit(solution)/shard_map/all_to_all | solution.py:38
  35.0 72.6 %collective-permute-start.7 = (bf16[256,1,128]{0,2,1:T(8,128)(2,1)}, bf16[256,1,128]{0,2,1:T(8,128)(2,1)}, u32[]{:S(2)}, u32[]{:S(2)}) collective-permute-start(bf16[256,1,128]{0,2,1:T(8,128)(2,1)} %copy.339), channel_id=1, source_target_pairs={{0,32},{8,40},{16,48},{24,56},{32,64},{40,72},{48,80},{56,88},{64,... | collective-permute-start | bytes 196616 | tf_op jit(solution)/shard_map/ppermute | solution.py:17
  40.2 62.8 %collective-permute-start.6 = (bf16[256,1,128]{0,2,1:T(8,128)(2,1)}, bf16[256,1,128]{0,2,1:T(8,128)(2,1)}, u32[]{:S(2)}, u32[]{:S(2)}) collective-permute-start(bf16[256,1,128]{0,2,1:T(8,128)(2,1)} %copy.339), channel_id=1, source_target_pairs={{0,24},{8,32},{16,40},{24,48},{32,56},{40,64},{48,72},{56,80},{64,... | collective-permute-start | bytes 196616 | tf_op jit(solution)/shard_map/ppermute | solution.py:17
  42.1 77.1 %collective-permute-start.5 = (bf16[256,1,128]{0,2,1:T(8,128)(2,1)}, bf16[256,1,128]{0,2,1:T(8,128)(2,1)S(1)}, u32[]{:S(2)}, u32[]{:S(2)}) collective-permute-start(bf16[256,1,128]{0,2,1:T(8,128)(2,1)} %copy.339), channel_id=1, source_target_pairs={{0,16},{8,24},{16,32},{24,40},{32,48},{40,56},{48,64},{56,72},{64,... | collective-permute-start | bytes 196616 | tf_op jit(solution)/shard_map/ppermute | solution.py:17
  46.2 53.2 %collective-permute-start.4 = (bf16[256,1,128]{0,2,1:T(8,128)(2,1)}, bf16[256,1,128]{0,2,1:T(8,128)(2,1)S(1)}, u32[]{:S(2)}, u32[]{:S(2)}) collective-permute-start(bf16[256,1,128]{0,2,1:T(8,128)(2,1)} %copy.339), channel_id=1, source_target_pairs={{0,8},{8,16},{16,24},{24,32},{32,40},{40,48},{48,56},{56,64},{64,7... | collective-permute-start | bytes 196616 | tf_op jit(solution)/shard_map/ppermute | solution.py:17
  52.2 9.7 %collective-permute-start = (bf16[256,1,128]{2,0,1:T(8,128)(2,1)S(1)}, bf16[256,1,128]{2,0,1:T(8,128)(2,1)}, u32[]{:S(2)}, u32[]{:S(2)}) collective-permute-start(bf16[256,1,128]{2,0,1:T(8,128)(2,1)S(1)} %bitcast.445), channel_id=1, source_target_pairs={{0,8},{8,16},{16,24},{24,32},{32,40},{40,48},{48,56},{56,64},{64,7... | collective-permute-start | bytes 196616 | tf_op jit(solution)/shard_map/ppermute | solution.py:17
  54.1 22.7 %all-to-all-start.4 = ((bf16[32,8,1024]{2,0,1:T(8,128)(2,1)}), bf16[32,8,1024]{2,0,1:T(8,128)(2,1)S(1)}, u32[]{:S(2)}, u32[]{:S(2)}) async-start(bf16[32,8,1024]{2,0,1:T(8,128)(2,1)} %bitcast.411), calls=%async_computation.4 | async-start | bytes 1048576 | tf_op jit(solution)/shard_map/all_to_all | solution.py:59
  61.3 4.4 %copy-start.19 = (pred[256,256]{0,1:T(8,128)(4,1)S(1)}, pred[256,256]{0,1:T(8,128)(4,1)}, u32[]{:S(2)}) copy-start(pred[256,256]{0,1:T(8,128)(4,1)} %get-tuple-element.15) | copy-start | bytes 196612
  61.4 13.1 %copy-start.18 = (pred[256,256]{0,1:T(8,128)(4,1)S(1)}, pred[256,256]{0,1:T(8,128)(4,1)}, u32[]{:S(2)}) copy-start(pred[256,256]{0,1:T(8,128)(4,1)} %get-tuple-element.19) | copy-start | bytes 196612
  61.9 8.3 %collective-permute-start.1 = (bf16[256,1,128]{2,0,1:T(8,128)(2,1)S(1)}, bf16[256,1,128]{2,0,1:T(8,128)(2,1)S(1)}, u32[]{:S(2)}, u32[]{:S(2)}) collective-permute-start(bf16[256,1,128]{2,0,1:T(8,128)(2,1)S(1)} %bitcast.447), channel_id=1, source_target_pairs={{0,16},{8,24},{16,32},{24,40},{32,48},{40,56},{48,64},{56,72},{64,... | collective-permute-start | bytes 196616 | tf_op jit(solution)/shard_map/ppermute | solution.py:17
  70.1 8.7 %collective-permute-start.2 = (bf16[256,1,128]{2,0,1:T(8,128)(2,1)S(1)}, bf16[256,1,128]{2,0,1:T(8,128)(2,1)}, u32[]{:S(2)}, u32[]{:S(2)}) collective-permute-start(bf16[256,1,128]{2,0,1:T(8,128)(2,1)S(1)} %bitcast.448), channel_id=1, source_target_pairs={{0,24},{8,32},{16,40},{24,48},{32,56},{40,64},{48,72},{56,80},{64,... | collective-permute-start | bytes 196616 | tf_op jit(solution)/shard_map/ppermute | solution.py:17
  76.8 4.9 %copy-start.17 = (pred[256,256]{0,1:T(8,128)(4,1)S(1)}, pred[256,256]{0,1:T(8,128)(4,1)}, u32[]{:S(2)}) copy-start(pred[256,256]{0,1:T(8,128)(4,1)} %get-tuple-element.16) | copy-start | bytes 196612
  78.9 9.8 %collective-permute-start.3 = (bf16[256,1,128]{2,0,1:T(8,128)(2,1)S(1)}, bf16[256,1,128]{2,0,1:T(8,128)(2,1)S(1)}, u32[]{:S(2)}, u32[]{:S(2)}) collective-permute-start(bf16[256,1,128]{2,0,1:T(8,128)(2,1)S(1)} %bitcast.449), channel_id=1, source_target_pairs={{0,32},{8,40},{16,48},{24,56},{32,64},{40,72},{48,80},{56,88},{64,... | collective-permute-start | bytes 196616 | tf_op jit(solution)/shard_map/ppermute | solution.py:17
  83.0 22.3 %copy-start.5 = (f32[1,8,256,256]{2,3,1,0:T(8,128)}, f32[1,8,256,256]{2,3,1,0:T(8,128)S(1)}, u32[]{:S(2)}) copy-start(f32[1,8,256,256]{2,3,1,0:T(8,128)S(1)} %get-tuple-element.23) | copy-start | bytes 6291460
  83.0 5.6 %copy-start.16 = (pred[256,256]{0,1:T(8,128)(4,1)S(1)}, pred[256,256]{0,1:T(8,128)(4,1)}, u32[]{:S(2)}) copy-start(pred[256,256]{0,1:T(8,128)(4,1)} %get-tuple-element.17) | copy-start | bytes 196612
  83.7 5.5 %copy-start.20 = (f32[8,256]{1,0:T(8,128)S(1)}, f32[8,256]{1,0:T(8,128)}, u32[]{:S(2)}) copy-start(f32[8,256]{1,0:T(8,128)} %get-tuple-element.24) | copy-start | bytes 24580
  88.7 0.8 copy-start.14
  89.2 23.1 %copy-start.7 = (f32[1,8,256,256]{2,3,1,0:T(8,128)}, f32[1,8,256,256]{2,3,1,0:T(8,128)S(1)}, u32[]{:S(2)}) copy-start(f32[1,8,256,256]{2,3,1,0:T(8,128)S(1)} %get-tuple-element.21) | copy-start | bytes 6291460
  89.2 2.3 %copy-start.3 = (f32[1,8,256,256]{2,3,1,0:T(8,128)S(1)}, f32[1,8,256,256]{2,3,1,0:T(8,128)}, u32[]{:S(2)}) copy-start(f32[1,8,256,256]{2,3,1,0:T(8,128)} %get-tuple-element.25) | copy-start | bytes 6291460
  89.5 2.6 %copy-start.1 = (f32[1,8,256,256]{2,3,1,0:T(8,128)S(1)}, f32[1,8,256,256]{2,3,1,0:T(8,128)}, u32[]{:S(2)}) copy-start(f32[1,8,256,256]{2,3,1,0:T(8,128)} %get-tuple-element.29) | copy-start | bytes 6291460
  97.5 44.7 %collective-permute-start.12 = (f32[256,1,128]{2,0,1:T(8,128)}, f32[256,1,128]{2,0,1:T(8,128)}, u32[]{:S(2)}, u32[]{:S(2)}) collective-permute-start(f32[256,1,128]{2,0,1:T(8,128)} %convolution_bitcast_fusion.3), channel_id=1, source_target_pairs={{8,0},{16,8},{24,16},{32,24},{40,32},{48,40},{56,48},{64,56},{72,6... | collective-permute-start | bytes 393224 | tf_op jit(solution)/shard_map/ppermute | solution.py:17
  99.5 46.0 %collective-permute-start.13 = (f32[256,1,128]{2,0,1:T(8,128)}, f32[256,1,128]{2,0,1:T(8,128)}, u32[]{:S(2)}, u32[]{:S(2)}) collective-permute-start(f32[256,1,128]{2,0,1:T(8,128)} %convolution_bitcast_fusion.2), channel_id=1, source_target_pairs={{16,0},{24,8},{32,16},{40,24},{48,32},{56,40},{64,48},{72,56},{80,... | collective-permute-start | bytes 393224 | tf_op jit(solution)/shard_map/ppermute | solution.py:17
  103.0 48.2 %collective-permute-start.14 = (f32[256,1,128]{2,0,1:T(8,128)}, f32[256,1,128]{2,0,1:T(8,128)}, u32[]{:S(2)}, u32[]{:S(2)}) collective-permute-start(f32[256,1,128]{2,0,1:T(8,128)} %convolution_bitcast_fusion.1), channel_id=1, source_target_pairs={{24,0},{32,8},{40,16},{48,24},{56,32},{64,40},{72,48},{80,56},{88,... | collective-permute-start | bytes 393224 | tf_op jit(solution)/shard_map/ppermute | solution.py:17
  107.6 46.1 %collective-permute-start.15 = (f32[256,1,128]{2,0,1:T(8,128)}, f32[256,1,128]{2,0,1:T(8,128)}, u32[]{:S(2)}, u32[]{:S(2)}) collective-permute-start(f32[256,1,128]{2,0,1:T(8,128)} %convolution_bitcast_fusion), channel_id=1, source_target_pairs={{32,0},{40,8},{48,16},{56,24},{64,32},{72,40},{80,48},{88,56},{96,... | collective-permute-start | bytes 393224 | tf_op jit(solution)/shard_map/ppermute | solution.py:17
  123.4 1.6 copy-start.8
  125.0 9.2 %copy-start.9 = (bf16[8,256,256]{1,2,0:T(8,128)(2,1)}, bf16[8,256,256]{1,2,0:T(8,128)(2,1)S(1)}, u32[]{:S(2)}) copy-start(bf16[8,256,256]{1,2,0:T(8,128)(2,1)S(1)} %fusion.20) | copy-start | bytes 3145732
  125.0 2.8 %copy-start.6 = (f32[1,8,256,256]{2,3,1,0:T(8,128)S(1)}, f32[1,8,256,256]{2,3,1,0:T(8,128)}, u32[]{:S(2)}) copy-start(f32[1,8,256,256]{2,3,1,0:T(8,128)} %copy-done.5) | copy-start | bytes 6291460
  127.8 2.7 %copy-start.2 = (f32[1,8,256,256]{2,3,1,0:T(8,128)S(1)}, f32[1,8,256,256]{2,3,1,0:T(8,128)}, u32[]{:S(2)}) copy-start(f32[1,8,256,256]{2,3,1,0:T(8,128)} %get-tuple-element.29) | copy-start | bytes 6291460
  131.2 3.4 %copy-start.4 = (f32[1,8,256,256]{2,3,1,0:T(8,128)S(1)}, f32[1,8,256,256]{2,3,1,0:T(8,128)}, u32[]{:S(2)}) copy-start(f32[1,8,256,256]{2,3,1,0:T(8,128)} %get-tuple-element.25) | copy-start | bytes 6291460
  132.2 31.2 %collective-permute-start.8 = (f32[256,1,128]{2,0,1:T(8,128)}, f32[256,1,128]{2,0,1:T(8,128)}, u32[]{:S(2)}, u32[]{:S(2)}) collective-permute-start(f32[256,1,128]{2,0,1:T(8,128)} %convolution_bitcast_fusion.8), channel_id=1, source_target_pairs={{8,0},{16,8},{24,16},{32,24},{40,32},{48,40},{56,48},{64,56},{72,6... | collective-permute-start | bytes 393224 | tf_op jit(solution)/shard_map/ppermute | solution.py:17
  134.6 0.8 copy-start.15
  135.4 5.7 %copy-start.10 = (bf16[8,256,256]{1,2,0:T(8,128)(2,1)}, bf16[8,256,256]{1,2,0:T(8,128)(2,1)S(1)}, u32[]{:S(2)}) copy-start(bf16[8,256,256]{1,2,0:T(8,128)(2,1)S(1)} %fusion.22) | copy-start | bytes 3145732
  142.2 21.2 %collective-permute-start.9 = (f32[256,1,128]{2,0,1:T(8,128)}, f32[256,1,128]{2,0,1:T(8,128)S(1)}, u32[]{:S(2)}, u32[]{:S(2)}) collective-permute-start(f32[256,1,128]{2,0,1:T(8,128)} %convolution_bitcast_fusion.7), channel_id=1, source_target_pairs={{16,0},{24,8},{32,16},{40,24},{48,32},{56,40},{64,48},{72,56},{80,... | collective-permute-start | bytes 393224 | tf_op jit(solution)/shard_map/ppermute | solution.py:17
  145.5 18.0 %collective-permute-start.10 = (f32[256,1,128]{2,0,1:T(8,128)}, f32[256,1,128]{2,0,1:T(8,128)}, u32[]{:S(2)}, u32[]{:S(2)}) collective-permute-start(f32[256,1,128]{2,0,1:T(8,128)} %convolution_bitcast_fusion.6), channel_id=1, source_target_pairs={{24,0},{32,8},{40,16},{48,24},{56,32},{64,40},{72,48},{80,56},{88,... | collective-permute-start | bytes 393224 | tf_op jit(solution)/shard_map/ppermute | solution.py:17
  151.2 12.3 %collective-permute-start.11 = (f32[256,1,128]{2,0,1:T(8,128)}, f32[256,1,128]{2,0,1:T(8,128)}, u32[]{:S(2)}, u32[]{:S(2)}) collective-permute-start(f32[256,1,128]{2,0,1:T(8,128)} %convolution_bitcast_fusion.5), channel_id=1, source_target_pairs={{32,0},{40,8},{48,16},{56,24},{64,32},{72,40},{80,48},{88,56},{96,... | collective-permute-start | bytes 393224 | tf_op jit(solution)/shard_map/ppermute | solution.py:17
  155.3 19.2 %copy-start.11 = (bf16[8,256,256]{1,2,0:T(8,128)(2,1)S(1)}, bf16[8,256,256]{1,2,0:T(8,128)(2,1)}, u32[]{:S(2)}) copy-start(bf16[8,256,256]{1,2,0:T(8,128)(2,1)} %copy-done.10) | copy-start | bytes 3145732
  155.3 19.2 %copy-start.12 = (f32[8,256,128]{1,2,0:T(8,128)S(1)}, f32[8,256,128]{1,2,0:T(8,128)}, u32[]{:S(2)}) copy-start(f32[8,256,128]{1,2,0:T(8,128)} %convolution_add_fusion.3) | copy-start | bytes 3145732
  157.2 14.0 %all-to-all-start.7 = ((bf16[8,2,2048]{2,1,0:T(2,128)(2,1)}), bf16[8,2,2048]{2,1,0:T(2,128)(2,1)S(1)}, u32[]{:S(2)}, u32[]{:S(2)}) async-start(bf16[8,2,2048]{2,1,0:T(2,128)(2,1)} %reshape.555), calls=%async_computation.7 | async-start | bytes 131072 | tf_op jit(solution)/shard_map/all_to_all | solution.py:185
  171.2 11.0 %all-to-all-start.6 = ((bf16[8,2,2048]{2,1,0:T(2,128)(2,1)}), bf16[8,2,2048]{2,1,0:T(2,128)(2,1)S(1)}, u32[]{:S(2)}, u32[]{:S(2)}) async-start(bf16[8,2,2048]{2,1,0:T(2,128)(2,1)} %reshape.553), calls=%async_computation.6 | async-start | bytes 131072 | tf_op jit(solution)/shard_map/all_to_all | solution.py:178
  176.6 9.5 %copy-start.13 = (bf16[8,256,128]{1,2,0:T(8,128)(2,1)S(1)}, bf16[8,256,128]{1,2,0:T(8,128)(2,1)}, u32[]{:S(2)}) copy-start(bf16[8,256,128]{1,2,0:T(8,128)(2,1)} %get-tuple-element.31) | copy-start | bytes 1572868
  182.3 13.5 %all-to-all-start.5 = ((bf16[8,2,16384]{2,1,0:T(2,128)(2,1)}), bf16[8,2,16384]{2,1,0:T(2,128)(2,1)S(1)}, u32[]{:S(2)}, u32[]{:S(2)}) async-start(bf16[8,2,16384]{2,1,0:T(2,128)(2,1)} %reshape.551), calls=%async_computation.5 | async-start | bytes 1048576 | tf_op jit(solution)/shard_map/all_to_all | solution.py:177
  195.8 13.1 %all-to-all-start.3 = ((bf16[8,2,16384]{2,1,0:T(2,128)(2,1)}), bf16[8,2,16384]{2,1,0:T(2,128)(2,1)S(1)}, u32[]{:S(2)}, u32[]{:S(2)}) async-start(bf16[8,2,16384]{2,1,0:T(2,128)(2,1)} %reshape.549), calls=%async_computation.3 | async-start | bytes 1048576 | tf_op jit(solution)/shard_map/all_to_all | solution.py:165
where the time goes:
time: 213 us; the launch traced here: 210 us
  starting transfers between devices  93.4 us (44%)
  matrix products  43.6 us (20%)
  waiting for transfers between devices  39.8 us (19%)
  local copies, waits for them, and re-layouts  25.6 us (12%)
  other arithmetic  6.69 us (3%)
    ppermute x16, starting transfers between devices, shifted(): return lax.ppermute(block, axis, route)  54.2 us
    unnamed x62, local copies, waits for them, and re-layouts  12.8 us
    dot_general x5, matrix products, shards(): jnp.einsum('agst,tad->sagd', weights, out_value_block, preferred_element_...  10.8 us
    ppermute x16, waiting for transfers between devices, shifted(): return lax.ppermute(block, axis, route)  8.48 us
    dot_general x5, matrix products, shards(): jnp.einsum('agst,tad->sagd', dscore, grad_key_block, preferred_element_ty...  8.06 us
    all_to_all x1, waiting for transfers between devices, shards(): lax.all_to_all(values.reshape(incoming_rows, head_groups, local_key_value...  7.76 us
    all_to_all x1, waiting for transfers between devices, shards(): lax.all_to_all(to_columns(query_grad_b), 'head', split_axis=0, concat_axi...  7.36 us
    dot_general x5, matrix products, score_block(): jnp.einsum('sagd,tad->agst', query_local, key_block, preferred_element_ty...  7.25 us
  transfers between devices with their start and end apart: 24, of which 9 were waited for; matrix products, arithmetic and copies ran while one was open for 33% of the time, Pallas kernels for 0%

commit v1 on v0

v1 whole, which is shorter than its diff:
```python
import math

import jax
import jax.numpy as jnp
from jax import lax
from jax.experimental import pallas as pl
from jax.experimental.pallas import tpu as pltpu
from jax.sharding import PartitionSpec as P

HEAD_WIDTH = 128
QUERY_HEADS = 64
KEY_VALUE_HEADS = 8
DOCS = 32
SHARDS = 64
GROUPS = 8
PER_GROUP = 8
PIECE = 32
SHARD = 256
WINDOW = 1280
REACH = 1152
CHUNK = 384
ROWS = PER_GROUP * PIECE
COLS = PER_GROUP * HEAD_WIDTH
SCALE = 1.0 / math.sqrt(HEAD_WIDTH)
SCALE2 = SCALE * math.log2(math.e)
MESH = pl.DeviceIdType.MESH
F32 = jnp.float32
BF16 = jnp.bfloat16


def dot_nn(a, b):
    return lax.dot_general(a, b, (((1,), (0,)), ((), ())), preferred_element_type=F32)


def dot_nt(a, b):
    return lax.dot_general(a, b, (((1,), (1,)), ((), ())), preferred_element_type=F32)


def stack_heads(piece):
    return jnp.concatenate(
        [piece[:, g * HEAD_WIDTH : (g + 1) * HEAD_WIDTH] for g in range(PER_GROUP)], axis=0
    )


def store_heads(ref, piece, rows):
    for g in range(PER_GROUP):
        ref[piece, :, g * HEAD_WIDTH : (g + 1) * HEAD_WIDTH] = rows[g * PIECE : (g + 1) * PIECE]


def attend(piece, shard_start, lens, qbuf, gbuf, kv, kv_t, obuf, dqbuf, acc, s_buf, dp_buf, p_buf):
    off = pl.multiple_of((piece // 4) * 128, 128)
    q_t = stack_heads(qbuf[piece]).T
    g_t = stack_heads(gbuf[piece]).T
    pos = shard_start + piece * PIECE + lax.rem(lax.broadcasted_iota(jnp.int32, (1, ROWS), 1), PIECE)
    start = jnp.zeros((1, ROWS), jnp.int32)
    end = jnp.int32(0)
    for n in range(DOCS):
        end = end + lens[n]
        start = jnp.where(pos >= end, end, start)
    first = shard_start - (WINDOW - SHARD) + off
    low = start - first
    high = pos - first
    top = jnp.full((1, ROWS), -jnp.inf, F32)
    for r in range(0, REACH, CHUNK):
        s = dot_nn(kv[0, pl.ds(off + r, CHUNK), :], q_t)
        at = lax.broadcasted_iota(jnp.int32, (CHUNK, ROWS), 0) + r
        allowed = at >= low
        if r + CHUNK > REACH - 128:
            allowed = allowed & (at <= high)
        s = jnp.where(allowed, s, -1e30)
        s_buf[r : r + CHUNK, :] = s
        top = jnp.maximum(top, jnp.max(s, axis=0, keepdims=True))
        dp_buf[r : r + CHUNK, :] = dot_nn(kv[1, pl.ds(off + r, CHUNK), :], g_t)
    total = jnp.zeros((1, ROWS), F32)
    o_t = jnp.zeros((HEAD_WIDTH, ROWS), F32)
    for r in range(0, REACH, CHUNK):
        p = jnp.exp2((s_buf[r : r + CHUNK, :] - top) * SCALE2)
        total = total + jnp.sum(p, axis=0, keepdims=True)
        p_b = p.astype(BF16)
        s_buf[r : r + CHUNK, :] = p
        p_buf[r : r + CHUNK, :] = p_b
        o_t = o_t + dot_nn(kv_t[1, :, pl.ds(pl.multiple_of(off + r, 128), CHUNK)], p_b)
    inv = 1.0 / total
    g_f = g_t.astype(F32)
    o_b = (o_t * inv).astype(BF16)
    delta = jnp.sum(g_f * o_b.astype(F32), axis=0, keepdims=True)
    g_n = (g_f * inv).astype(BF16)
    q_n = (q_t.astype(F32) * inv).astype(BF16)
    store_heads(obuf, piece, o_b.T)
    dq_t = jnp.zeros((HEAD_WIDTH, ROWS), F32)
    for r in range(0, REACH, CHUNK):
        ds = (s_buf[r : r + CHUNK, :] * (dp_buf[r : r + CHUNK, :] - delta)).astype(BF16)
        dq_t = dq_t + dot_nn(kv_t[0, :, pl.ds(pl.multiple_of(off + r, 128), CHUNK)], ds)
        acc[0, pl.ds(off + r, CHUNK), :] += dot_nt(ds, q_n)
        acc[1, pl.ds(off + r, CHUNK), :] += dot_nt(p_buf[r : r + CHUNK, :], g_n)
    store_heads(dqbuf, piece, (dq_t * (inv * SCALE)).astype(BF16).T)


def kernel(
    q_in, k_in, v_in, g_in, lens,
    o_out, dq_out, dk_out, dv_out,
    qbuf, gbuf, kv, kv_t, obuf, dqbuf, acc, s_buf, dp_buf, p_buf,
    swap_out, swap_in, far_out, far_in, last,
    q_sem, g_sem, kv_sem, fwd_sem, swap_sem, back_sem, far_sem,
    o_sem, dq_sem, dk_sem, dv_sem, send_sem,
):
    c = lax.axis_index("ctx")
    me = lax.axis_index("head")
    core = lax.rem(c, 2)
    other = (c + 1 - 2 * core, me)
    along = {d: (lax.rem(c + d + SHARDS, SHARDS), me) for d in (2, 4, -2, -4)}
    peers = [lax.rem(me + i, GROUPS) for i in range(GROUPS)]
    takers = [lax.rem(me - i + GROUPS, GROUPS) for i in range(GROUPS)]
    own = slice(WINDOW - SHARD, WINDOW)

    def columns(h, width):
        return pl.ds(pl.multiple_of(h * width, width), width)

    def rows_of(h):
        return pl.ds(pl.multiple_of(WINDOW - SHARD + h * PIECE, PIECE), PIECE)

    local = [
        pltpu.make_async_copy(k_in.at[:, columns(me, HEAD_WIDTH)], kv.at[0, rows_of(me)], kv_sem),
        pltpu.make_async_copy(v_in.at[:, columns(me, HEAD_WIDTH)], kv.at[1, rows_of(me)], kv_sem),
        pltpu.make_async_copy(q_in.at[:, columns(me, COLS)], qbuf.at[me], q_sem.at[0]),
        pltpu.make_async_copy(g_in.at[:, columns(me, COLS)], gbuf.at[me], g_sem.at[0]),
    ]
    for copy in local:
        copy.start()

    barrier = pltpu.get_barrier_semaphore()
    partners = [(c, peers[i]) for i in range(1, GROUPS)] + [other] + list(along.values())
    for partner in partners:
        pl.semaphore_signal(barrier, inc=1, device_id=partner, device_id_type=MESH)
    pl.semaphore_wait(barrier, len(partners))

    def send(src, dst, sent, landed, to):
        pltpu.make_async_remote_copy(
            src_ref=src, dst_ref=dst, send_sem=sent, recv_sem=landed, device_id=to, device_id_type=MESH
        ).start()

    def landed(ref, sem):
        pltpu.make_async_copy(ref, ref, sem).wait()

    for i in range(1, GROUPS):
        to = (c, takers[i])
        send(k_in.at[:, columns(takers[i], HEAD_WIDTH)], kv.at[0, rows_of(me)], send_sem.at[0], kv_sem, to)
        send(v_in.at[:, columns(takers[i], HEAD_WIDTH)], kv.at[1, rows_of(me)], send_sem.at[0], kv_sem, to)
    for i in range(1, GROUPS):
        to = (c, takers[i])
        send(q_in.at[:, columns(takers[i], COLS)], qbuf.at[me], send_sem.at[1], q_sem.at[i], to)
        send(g_in.at[:, columns(takers[i], COLS)], gbuf.at[me], send_sem.at[2], g_sem.at[i], to)

    acc[...] = jnp.zeros_like(acc)

    def back(distance):
        return pl.ds(pl.multiple_of((4 - distance) * SHARD, SHARD), SHARD)

    landed(kv.at[:, own], kv_sem)
    send(kv.at[:, own], kv.at[:, back(2)], send_sem.at[3], fwd_sem.at[0], along[2])
    send(kv.at[:, own], kv.at[:, back(4)], send_sem.at[4], fwd_sem.at[1], along[4])
    landed(kv.at[:, back(2)], fwd_sem.at[0])
    send(kv.at[:, back(2 * core)], kv.at[:, back(1)], send_sem.at[5], swap_sem.at[0], other)
    landed(kv.at[:, back(4)], fwd_sem.at[1])
    send(kv.at[:, back(2 * core + 2)], kv.at[:, back(3)], send_sem.at[6], swap_sem.at[1], other)
    landed(kv.at[:, back(1)], swap_sem.at[0])
    landed(kv.at[:, back(3)], swap_sem.at[1])
    kv_t[0] = kv[0].T
    kv_t[1] = kv[1].T

    def step(i, carry):
        peer = lax.rem(me + i, GROUPS)
        landed(qbuf.at[peer], q_sem.at[i])
        landed(gbuf.at[peer], g_sem.at[i])
        attend(peer, c * SHARD, lens, qbuf, gbuf, kv, kv_t, obuf, dqbuf, acc, s_buf, dp_buf, p_buf)

        @pl.when(i == 0)
        def _():
            pltpu.make_async_copy(obuf.at[me], o_out.at[:, columns(me, COLS)], o_sem).start()
            pltpu.make_async_copy(dqbuf.at[me], dq_out.at[:, columns(me, COLS)], dq_sem).start()

        @pl.when(i > 0)
        def _():
            send(obuf.at[peer], o_out.at[:, columns(me, COLS)], send_sem.at[7], o_sem, (c, peer))
            send(dqbuf.at[peer], dq_out.at[:, columns(me, COLS)], send_sem.at[8], dq_sem, (c, peer))

        return carry

    lax.fori_loop(0, GROUPS, step, 0)

    def part(distance):
        rows = slice((4 - distance) * SHARD, (5 - distance) * SHARD)
        return jnp.stack([acc[0, rows, :] * SCALE, acc[1, rows, :]])

    swap_out[0] = part(1).astype(BF16)
    swap_out[1] = part(3).astype(BF16)
    send(swap_out, swap_in, send_sem.at[9], back_sem, other)
    landed(swap_in, back_sem)
    from_near = swap_in[0].astype(F32)
    from_far = swap_in[1].astype(F32)
    zero = jnp.zeros_like(from_near)
    first_core = core == 0
    far_out[1] = (part(4) + jnp.where(first_core, zero, from_far)).astype(BF16)
    send(far_out.at[1], far_in.at[1], send_sem.at[10], far_sem.at[1], along[-4])
    far_out[0] = (part(2) + jnp.where(first_core, from_far, from_near)).astype(BF16)
    send(far_out.at[0], far_in.at[0], send_sem.at[11], far_sem.at[0], along[-2])
    base = part(0) + jnp.where(first_core, from_near, zero)
    landed(far_in.at[0], far_sem.at[0])
    landed(far_in.at[1], far_sem.at[1])
    last[...] = (base + far_in[0].astype(F32) + far_in[1].astype(F32)).astype(BF16)

    def piece_of(h):
        return pl.ds(pl.multiple_of(h * PIECE, PIECE), PIECE)

    mine = columns(me, HEAD_WIDTH)
    pltpu.make_async_copy(last.at[0, piece_of(me)], dk_out.at[:, mine], dk_sem).start()
    pltpu.make_async_copy(last.at[1, piece_of(me)], dv_out.at[:, mine], dv_sem).start()
    for i in range(1, GROUPS):
        to = (c, peers[i])
        send(last.at[0, piece_of(peers[i])], dk_out.at[:, mine], send_sem.at[12], dk_sem, to)
        send(last.at[1, piece_of(peers[i])], dv_out.at[:, mine], send_sem.at[13], dv_sem, to)

    others = pl.ds(0, GROUPS - 1)
    landed(o_out, o_sem)
    landed(dq_out, dq_sem)
    landed(dk_out, dk_sem)
    landed(dv_out, dv_sem)
    landed(kv.at[:, pl.ds(0, (GROUPS - 1) * PIECE)], send_sem.at[0])
    for sem, ref in ((1, qbuf), (2, gbuf), (7, obuf), (8, dqbuf)):
        landed(ref.at[others], send_sem.at[sem])
    for sem in (3, 4, 5, 6):
        landed(kv.at[:, own], send_sem.at[sem])
    landed(swap_out, send_sem.at[9])
    landed(far_out.at[1], send_sem.at[10])
    landed(far_out.at[0], send_sem.at[11])
    landed(last.at[0, pl.ds(0, (GROUPS - 1) * PIECE)], send_sem.at[12])
    landed(last.at[1, pl.ds(0, (GROUPS - 1) * PIECE)], send_sem.at[13])


def shards(queries, keys, values, output_gradient, doc_lengths):
    hbm = pl.BlockSpec(memory_space=pl.ANY)
    dma = pltpu.SemaphoreType.DMA
    wide = (GROUPS, PIECE, COLS)
    pair = (2, 2, SHARD, HEAD_WIDTH)
    return pl.pallas_call(
        kernel,
        out_shape=[jax.ShapeDtypeStruct(a.shape, BF16) for a in (queries, queries, keys, values)],
        in_specs=[hbm] * 4 + [pl.BlockSpec(memory_space=pltpu.SMEM)],
        out_specs=[hbm] * 4,
        scratch_shapes=[
            pltpu.VMEM(wide, BF16),
            pltpu.VMEM(wide, BF16),
            pltpu.VMEM((2, WINDOW, HEAD_WIDTH), BF16),
            pltpu.VMEM((2, HEAD_WIDTH, WINDOW), BF16),
            pltpu.VMEM(wide, BF16),
            pltpu.VMEM(wide, BF16),
            pltpu.VMEM((2, WINDOW, HEAD_WIDTH), F32),
            pltpu.VMEM((REACH, ROWS), F32),
            pltpu.VMEM((REACH, ROWS), F32),
            pltpu.VMEM((REACH, ROWS), BF16),
            pltpu.VMEM(pair, BF16),
            pltpu.VMEM(pair, BF16),
            pltpu.VMEM(pair, BF16),
            pltpu.VMEM(pair, BF16),
            pltpu.VMEM((2, SHARD, HEAD_WIDTH), BF16),
            dma((GROUPS,)),
            dma((GROUPS,)),
            dma,
            dma((2,)),
            dma((2,)),
            dma,
            dma((2,)),
            dma,
            dma,
            dma,
            dma,
            dma((14,)),
        ],
        compiler_params=pltpu.CompilerParams(
            collective_id=0, has_side_effects=True, vmem_limit_bytes=50 * 2**20
        ),
    )(queries, keys, values, output_gradient, doc_lengths)


def solution(mesh):
    rows = P(("ctx", "head"), None)
    return jax.shard_map(
        shards,
        mesh=mesh,
        in_specs=(rows, rows, rows, rows, P()),
        out_specs=(rows, rows, rows, rows),
        check_vma=False,
    )
```

time: 213 us -> 75.2 us (0.35)
  the two profiles are of different devices: /device:TPU:8 before, /device:TPU:1 now
where the time goes in v1:
time: 75.2 us; the launch traced here: 74.9 us
  Pallas kernels  67 us (89%)
  local copies, waits for them, and re-layouts  7.25 us (10%)
    pallas_call x1, Pallas kernels, shards(): pl.pallas_call(kernel, out_shape=[jax.ShapeDtypeStruct(a.shape, BF16) for...  67 us
    unnamed x14, local copies, waits for them, and re-layouts  7.25 us

profile of v1, /device:TPU:1, one launch (start us, length us, event | category | flops | bytes accessed | tf_op | source)
XLA Modules:
  0.0 74.9 jit_solution(15961107874037841527)
XLA Ops:
  0.6 0.0 copy-start
  0.6 1.0 %copy-done = bf16[32,8192]{1,0:T(8,128)(2,1)S(1)} copy-done((bf16[32,8192]{1,0:T(8,128)(2,1)S(1)}, bf16[32,8192]{1,0:T(8,128)(2,1)}, u32[]{:S(2)}) %copy-start) | copy-done | bytes 524312
  1.7 0.0 copy-start.1
  1.7 1.0 %copy-done.1 = bf16[32,8192]{1,0:T(8,128)(2,1)S(1)} copy-done((bf16[32,8192]{1,0:T(8,128)(2,1)S(1)}, bf16[32,8192]{1,0:T(8,128)(2,1)}, u32[]{:S(2)}) %copy-start.1) | copy-done | bytes 524312
  2.7 0.0 copy-start.2
  2.7 0.8 %copy-done.2 = bf16[32,1024]{1,0:T(8,128)(2,1)S(1)} copy-done((bf16[32,1024]{1,0:T(8,128)(2,1)S(1)}, bf16[32,1024]{1,0:T(8,128)(2,1)}, u32[]{:S(2)}) %copy-start.2) | copy-done | bytes 65560
  3.6 0.0 copy-start.3
  3.6 0.8 %copy-done.3 = bf16[32,1024]{1,0:T(8,128)(2,1)S(1)} copy-done((bf16[32,1024]{1,0:T(8,128)(2,1)S(1)}, bf16[32,1024]{1,0:T(8,128)(2,1)}, u32[]{:S(2)}) %copy-start.3) | copy-done | bytes 65560
  4.4 0.0 copy-start.4
  4.4 0.7 copy-done.4
  5.1 67.0 %shard_map.84 = (bf16[32,8192]{1,0:T(8,128)(2,1)S(1)}, bf16[32,8192]{1,0:T(8,128)(2,1)S(1)}, bf16[32,1024]{1,0:T(8,128)(2,1)S(1)}, bf16[32,1024]{1,0:T(8,128)(2,1)S(1)}) custom-call(bf16[32,8192]{1,0:T(8,128)(2,1)S(1)} %copy-done, bf16[32,1024]{1,0:T(8,128)(2,1)S(1)} %copy-done.2, bf16[32,1024]{1,0:T(8,128)(2,1)S(1)} %copy-done.3, ...), custom_call_target="tpu_custom_call" | custom-call | tf_op jit(solution)/shard_map/pallas_call | solution.py:245
  72.0 0.8 %copy.13 = bf16[32,8192]{1,0:T(8,128)(2,1)} copy(bf16[32,8192]{1,0:T(8,128)(2,1)S(1)} %get-tuple-element.8) | data formatting | bytes 1048576
  72.8 0.8 %copy.14 = bf16[32,8192]{1,0:T(8,128)(2,1)} copy(bf16[32,8192]{1,0:T(8,128)(2,1)S(1)} %get-tuple-element.9) | data formatting | bytes 1048576
  73.6 0.6 copy.15
  74.2 0.6 copy.16
Async XLA Ops:
  0.6 1.0 %copy-start = (bf16[32,8192]{1,0:T(8,128)(2,1)S(1)}, bf16[32,8192]{1,0:T(8,128)(2,1)}, u32[]{:S(2)}) copy-start(bf16[32,8192]{1,0:T(8,128)(2,1)} %q_in.1) | copy-start | bytes 1572868
  1.7 1.0 %copy-start.1 = (bf16[32,8192]{1,0:T(8,128)(2,1)S(1)}, bf16[32,8192]{1,0:T(8,128)(2,1)}, u32[]{:S(2)}) copy-start(bf16[32,8192]{1,0:T(8,128)(2,1)} %g_in.1) | copy-start | bytes 1572868
  2.7 0.8 %copy-start.2 = (bf16[32,1024]{1,0:T(8,128)(2,1)S(1)}, bf16[32,1024]{1,0:T(8,128)(2,1)}, u32[]{:S(2)}) copy-start(bf16[32,1024]{1,0:T(8,128)(2,1)} %k_in.1) | copy-start | bytes 196612
  3.6 0.8 %copy-start.3 = (bf16[32,1024]{1,0:T(8,128)(2,1)S(1)}, bf16[32,1024]{1,0:T(8,128)(2,1)}, u32[]{:S(2)}) copy-start(bf16[32,1024]{1,0:T(8,128)(2,1)} %v_in.1) | copy-start | bytes 196612
  4.4 0.7 copy-start.4

commit v2 on v1

v2 whole, which is shorter than its diff:
```python
import math

import jax
import jax.numpy as jnp
from jax import lax
from jax.experimental import pallas as pl
from jax.experimental.pallas import tpu as pltpu
from jax.sharding import PartitionSpec as P

HEAD_WIDTH = 128
DOCS = 32
SHARDS = 64
GROUPS = 8
PER_GROUP = 8
PIECE = 32
SHARD = 256
WINDOW = 1280
REACH = 1152
ROWS = PER_GROUP * PIECE
COLS = PER_GROUP * HEAD_WIDTH
SCALE = 1.0 / math.sqrt(HEAD_WIDTH)
SCALE2 = SCALE * math.log2(math.e)
MESH = pl.DeviceIdType.MESH
F32 = jnp.float32
BF16 = jnp.bfloat16


def dot_nn(a, b):
    return lax.dot_general(a, b, (((1,), (0,)), ((), ())), preferred_element_type=F32)


def dot_nt(a, b):
    return lax.dot_general(a, b, (((1,), (1,)), ((), ())), preferred_element_type=F32)


def heads_t(piece):
    rows = [piece[:, g * HEAD_WIDTH : (g + 1) * HEAD_WIDTH] for g in range(PER_GROUP)]
    return jnp.concatenate(rows, axis=0).T


def store_heads(ref, piece, which, rows):
    for g in range(PER_GROUP):
        cols = slice(g * HEAD_WIDTH, (g + 1) * HEAD_WIDTH)
        ref[piece, which, :, cols] = rows[g * PIECE : (g + 1) * PIECE]


def piece_scores(piece, shard_start, lens, qg, kv, s_buf, dp_buf):
    off = pl.multiple_of((piece // 4) * 128, 128)
    q_t = heads_t(qg[piece, 0])
    g_t = heads_t(qg[piece, 1])
    pos = shard_start + piece * PIECE + lax.rem(lax.broadcasted_iota(jnp.int32, (1, ROWS), 1), PIECE)
    start = jnp.zeros((1, ROWS), jnp.int32)
    end = jnp.int32(0)
    for n in range(DOCS):
        end = end + lens[n]
        start = jnp.where(pos >= end, end, start)
    first = shard_start - (WINDOW - SHARD) + off
    edge = REACH - 128
    s = dot_nn(kv[0, pl.ds(off, REACH), :], q_t)
    at = lax.broadcasted_iota(jnp.int32, (REACH, ROWS), 0)
    late = at >= start - first
    early_s = jnp.where(late[:edge], s[:edge], -1e30)
    last_s = jnp.where(late[edge:] & (at[edge:] <= pos - first), s[edge:], -1e30)
    s_buf[:edge, :] = early_s
    s_buf[edge:, :] = last_s
    top = jnp.maximum(jnp.max(early_s, axis=0, keepdims=True), jnp.max(last_s, axis=0, keepdims=True))
    dp_buf[...] = dot_nn(kv[1, pl.ds(off, REACH), :], g_t)
    return off, q_t, g_t, top


def piece_forward(piece, scored, kv_t, odq, s_buf, p_buf):
    off, q_t, g_t, top = scored
    p = jnp.exp2((s_buf[...] - top) * SCALE2)
    total = jnp.sum(p, axis=0, keepdims=True)
    p_b = p.astype(BF16)
    s_buf[...] = p
    p_buf[...] = p_b
    o_t = dot_nn(kv_t[1, :, pl.ds(off, REACH)], p_b)
    inv = 1.0 / total
    g_f = g_t.astype(F32)
    o_b = (o_t * inv).astype(BF16)
    delta = jnp.sum(g_f * o_b.astype(F32), axis=0, keepdims=True)
    g_n = (g_f * inv).astype(BF16)
    q_n = (q_t.astype(F32) * inv).astype(BF16)
    store_heads(odq, piece, 0, o_b.T)
    return off, inv, delta, g_n, q_n


def piece_backward(piece, done, kv_t, odq, acc, s_buf, dp_buf, p_buf):
    off, inv, delta, g_n, q_n = done
    ds = (s_buf[...] * (dp_buf[...] - delta)).astype(BF16)
    dq_t = dot_nn(kv_t[0, :, pl.ds(off, REACH)], ds)
    acc[0, pl.ds(off, REACH), :] += dot_nt(ds, q_n)
    acc[1, pl.ds(off, REACH), :] += dot_nt(p_buf[...], g_n)
    store_heads(odq, piece, 1, (dq_t * (inv * SCALE)).astype(BF16).T)


def kernel(
    q_in, k_in, v_in, g_in, lens,
    odq_out, dkv_out,
    qg_own, kv_own, qg, kv, kv_t, odq, acc, s_buf, dp_buf, p_buf,
    swap_out, swap_in, far_out, far_in, last,
    stage_sem, qg_sem, kv_sem, fwd_sem, swap_sem, back_sem, far_sem, odq_sem, dkv_sem, send_sem,
):
    c = lax.axis_index("ctx")
    me = lax.axis_index("head")
    core = lax.rem(c, 2)
    other = (c + 1 - 2 * core, me)
    ahead = (lax.rem(c + 2, SHARDS), me)
    behind = (lax.rem(c + SHARDS - 2, SHARDS), me)
    peers = [lax.rem(me + i, GROUPS) for i in range(GROUPS)]
    takers = [lax.rem(me - i + GROUPS, GROUPS) for i in range(GROUPS)]
    own = slice(WINDOW - SHARD, WINDOW)

    def columns(h, width):
        return pl.ds(pl.multiple_of(h * width, width), width)

    def rows_of(h):
        return pl.ds(pl.multiple_of(WINDOW - SHARD + h * PIECE, PIECE), PIECE)

    def back(distance):
        return pl.ds(pl.multiple_of((4 - distance) * SHARD, SHARD), SHARD)

    def local(src, dst, sem):
        pltpu.make_async_copy(src, dst, sem).start()

    def send(src, dst, sent, arrived, to):
        pltpu.make_async_remote_copy(
            src_ref=src, dst_ref=dst, send_sem=sent, recv_sem=arrived, device_id=to, device_id_type=MESH
        ).start()

    def landed(ref, sem):
        pltpu.make_async_copy(ref, ref, sem).wait()

    local(k_in, kv_own.at[0], stage_sem.at[0])
    local(v_in, kv_own.at[1], stage_sem.at[0])
    local(q_in, qg_own.at[0], stage_sem.at[1])
    local(g_in, qg_own.at[1], stage_sem.at[1])
    local(k_in.at[:, columns(me, HEAD_WIDTH)], kv.at[0, rows_of(me)], kv_sem)
    local(v_in.at[:, columns(me, HEAD_WIDTH)], kv.at[1, rows_of(me)], kv_sem)
    local(q_in.at[:, columns(me, COLS)], qg.at[me, 0], qg_sem.at[0])
    local(g_in.at[:, columns(me, COLS)], qg.at[me, 1], qg_sem.at[0])

    barrier = pltpu.get_barrier_semaphore()
    partners = [(c, peers[i]) for i in range(1, GROUPS)] + [other, ahead, behind]
    for partner in partners:
        pl.semaphore_signal(barrier, inc=1, device_id=partner, device_id_type=MESH)
    acc[...] = jnp.zeros_like(acc)
    landed(kv_own, stage_sem.at[0])
    landed(qg_own, stage_sem.at[1])
    pl.semaphore_wait(barrier, len(partners))

    for i in range(1, GROUPS):
        cols = columns(takers[i], HEAD_WIDTH)
        send(kv_own.at[:, :, cols], kv.at[:, rows_of(me)], send_sem.at[0], kv_sem, (c, takers[i]))
    for i in range(1, GROUPS):
        cols = columns(takers[i], COLS)
        send(qg_own.at[:, :, cols], qg.at[me], send_sem.at[1], qg_sem.at[i], (c, takers[i]))

    landed(kv.at[:, own], kv_sem)
    for n in range(2):
        send(kv.at[n, own], kv.at[n, back(2)], send_sem.at[2], fwd_sem.at[n], ahead)
    for n in range(2):
        kv_t[n, :, own] = kv[n, own, :].T
    for n in range(2):
        landed(kv.at[n, back(2)], fwd_sem.at[n])
        send(kv.at[n, back(2)], kv.at[n, back(4)], send_sem.at[3], fwd_sem.at[2 + n], ahead)
        send(kv.at[n, back(2 * core)], kv.at[n, back(1)], send_sem.at[4], swap_sem.at[n], other)
    for n in range(2):
        kv_t[n, :, 512:768] = kv[n, 512:768, :].T
    for n in range(2):
        landed(kv.at[n, back(1)], swap_sem.at[n])
        kv_t[n, :, 768:1024] = kv[n, 768:1024, :].T
    for n in range(2):
        landed(kv.at[n, back(4)], fwd_sem.at[2 + n])
        send(kv.at[n, back(2 * core + 2)], kv.at[n, back(3)], send_sem.at[5], swap_sem.at[2 + n], other)
    for n in range(2):
        kv_t[n, :, 0:256] = kv[n, 0:256, :].T
    for n in range(2):
        landed(kv.at[n, back(3)], swap_sem.at[2 + n])
        kv_t[n, :, 256:512] = kv[n, 256:512, :].T

    def step(i, carry):
        pair = [lax.rem(me + 2 * i + n, GROUPS) for n in range(2)]
        for n in range(2):
            landed(qg.at[pair[n]], qg_sem.at[2 * i + n])
        scored = [
            piece_scores(pair[n], c * SHARD, lens, qg, kv, s_buf.at[n], dp_buf.at[n]) for n in range(2)
        ]
        done = [piece_forward(pair[n], scored[n], kv_t, odq, s_buf.at[n], p_buf.at[n]) for n in range(2)]
        for n in range(2):
            piece_backward(pair[n], done[n], kv_t, odq, acc, s_buf.at[n], dp_buf.at[n], p_buf.at[n])
        mine = odq_out.at[:, :, columns(me, COLS)]

        @pl.when(i == 0)
        def _():
            local(odq.at[pair[0]], mine, odq_sem)

        @pl.when(i > 0)
        def _():
            send(odq.at[pair[0]], mine, send_sem.at[6], odq_sem, (c, pair[0]))

        send(odq.at[pair[1]], mine, send_sem.at[6], odq_sem, (c, pair[1]))
        return carry

    lax.fori_loop(0, GROUPS // 2, step, 0)

    def part(n, distance):
        rows = acc[n, (4 - distance) * SHARD : (5 - distance) * SHARD, :]
        return rows * SCALE if n == 0 else rows

    first_core = core == 0
    for m, distance in ((1, 3), (0, 1)):
        for n in range(2):
            swap_out[m, n] = part(n, distance).astype(BF16)
        send(swap_out.at[m], swap_in.at[m], send_sem.at[7 + m], back_sem.at[m], other)
    landed(swap_in.at[1], back_sem.at[1])
    for n in range(2):
        add = jnp.where(first_core, 0.0, swap_in[1, n].astype(F32))
        far_out[1, n] = (part(n, 4) + add).astype(BF16)
        send(far_out.at[1, n], far_in.at[1, n], send_sem.at[9], far_sem.at[n], behind)
    landed(swap_in.at[0], back_sem.at[0])
    for n in range(2):
        near = part(n, 2) + jnp.where(first_core, swap_in[1, n], swap_in[0, n]).astype(F32)
        landed(far_in.at[1, n], far_sem.at[n])
        far_out[0, n] = (near + far_in[1, n].astype(F32)).astype(BF16)
        send(far_out.at[0, n], far_in.at[0, n], send_sem.at[10], far_sem.at[2 + n], behind)
    for n in range(2):
        base = part(n, 0) + jnp.where(first_core, swap_in[0, n].astype(F32), 0.0)
        landed(far_in.at[0, n], far_sem.at[2 + n])
        last[n] = (base + far_in[0, n].astype(F32)).astype(BF16)

    def piece_of(h):
        return last.at[:, pl.ds(pl.multiple_of(h * PIECE, PIECE), PIECE)]

    mine = dkv_out.at[:, :, columns(me, HEAD_WIDTH)]
    for i in range(1, GROUPS):
        send(piece_of(peers[i]), mine, send_sem.at[11], dkv_sem, (c, peers[i]))
    local(piece_of(me), mine, dkv_sem)

    others = pl.ds(0, GROUPS - 1)
    landed(kv.at[:, pl.ds(0, (GROUPS - 1) * PIECE)], send_sem.at[0])
    landed(qg.at[others], send_sem.at[1])
    for sem in (2, 3, 4, 5):
        landed(kv.at[:, own], send_sem.at[sem])
    landed(odq.at[others], send_sem.at[6])
    landed(swap_out.at[0], send_sem.at[7])
    landed(swap_out.at[1], send_sem.at[8])
    landed(far_out.at[1], send_sem.at[9])
    landed(far_out.at[0], send_sem.at[10])
    landed(last.at[:, pl.ds(0, (GROUPS - 1) * PIECE)], send_sem.at[11])
    landed(odq_out, odq_sem)
    landed(dkv_out, dkv_sem)


def write(odq, dkv, o_out, dq_out, dk_out, dv_out, odq_buf, dkv_buf, in_sem, out_sem):
    steps = [
        (odq.at[0], odq_buf.at[0], o_out),
        (odq.at[1], odq_buf.at[1], dq_out),
        (dkv.at[0], dkv_buf.at[0], dk_out),
        (dkv.at[1], dkv_buf.at[1], dv_out),
    ]
    reads = [pltpu.make_async_copy(src, buf, in_sem.at[n]) for n, (src, buf, _) in enumerate(steps)]
    writes = [pltpu.make_async_copy(buf, dst, out_sem.at[n]) for n, (_, buf, dst) in enumerate(steps)]
    for copy in reads:
        copy.start()
    for n in range(len(steps)):
        reads[n].wait()
        writes[n].start()
    for copy in writes:
        copy.wait()


def shards(queries, keys, values, output_gradient, doc_lengths):
    hbm = pl.BlockSpec(memory_space=pl.ANY)
    dma = pltpu.SemaphoreType.DMA
    vmem = pltpu.VMEM
    wide = queries.shape
    narrow = keys.shape
    swap = (2, 2, SHARD, HEAD_WIDTH)
    odq, dkv = pl.pallas_call(
        kernel,
        out_shape=[jax.ShapeDtypeStruct((2, *wide), BF16), jax.ShapeDtypeStruct((2, *narrow), BF16)],
        in_specs=[hbm] * 4 + [pl.BlockSpec(memory_space=pltpu.SMEM)],
        out_specs=[hbm] * 2,
        scratch_shapes=[
            vmem((2, *wide), BF16),
            vmem((2, *narrow), BF16),
            vmem((GROUPS, 2, PIECE, COLS), BF16),
            vmem((2, WINDOW, HEAD_WIDTH), BF16),
            vmem((2, HEAD_WIDTH, WINDOW), BF16),
            vmem((GROUPS, 2, PIECE, COLS), BF16),
            vmem((2, WINDOW, HEAD_WIDTH), F32),
            vmem((2, REACH, ROWS), F32),
            vmem((2, REACH, ROWS), F32),
            vmem((2, REACH, ROWS), BF16),
            vmem(swap, BF16),
            vmem(swap, BF16),
            vmem(swap, BF16),
            vmem(swap, BF16),
            vmem((2, SHARD, HEAD_WIDTH), BF16),
            dma((2,)),
            dma((GROUPS,)),
            dma,
            dma((4,)),
            dma((4,)),
            dma((2,)),
            dma((4,)),
            dma,
            dma,
            dma((12,)),
        ],
        compiler_params=pltpu.CompilerParams(
            collective_id=0, has_side_effects=True, vmem_limit_bytes=63 * 2**20
        ),
    )(queries, keys, values, output_gradient, doc_lengths)
    return pl.pallas_call(
        write,
        out_shape=[jax.ShapeDtypeStruct(shape, BF16) for shape in (wide, wide, narrow, narrow)],
        in_specs=[hbm] * 2,
        out_specs=[hbm] * 4,
        scratch_shapes=[vmem((2, *wide), BF16), vmem((2, *narrow), BF16), dma((4,)), dma((4,))],
        compiler_params=pltpu.CompilerParams(vmem_limit_bytes=63 * 2**20),
    )(odq, dkv)


def solution(mesh):
    rows = P(("ctx", "head"), None)
    return jax.shard_map(
        shards,
        mesh=mesh,
        in_specs=(rows, rows, rows, rows, P()),
        out_specs=(rows, rows, rows, rows),
        check_vma=False,
    )
```

time: 75.2 us -> 64.8 us (0.86)
  local copies, waits for them, and re-layouts: 7.25 us -> 0 us
  Pallas kernels: 67 us -> 63.1 us
    unnamed x14 -> x0, local copies, waits for them, and re-layouts: 7.25 us -> none
    pallas_call x1 -> x2, Pallas kernels: 67 us -> 63.1 us  [the longest x1 61 us: shards(): pl.pallas_call(kernel, out_shape=[jax.ShapeDtypeStruct((2, *wide), BF16),...]
where the time goes in v2:
time: 64.8 us; the launch traced here: 63.7 us
  Pallas kernels  63.1 us (97%)
    pallas_call x1, Pallas kernels, shards(): pl.pallas_call(kernel, out_shape=[jax.ShapeDtypeStruct((2, *wide), BF16),...  61 us
    pallas_call x1, Pallas kernels, shards(): pl.pallas_call(write, out_shape=[jax.ShapeDtypeStruct(shape, BF16) for sh...  2.11 us

profile of v2, /device:TPU:1, one launch (start us, length us, event | category | flops | bytes accessed | tf_op | source)
XLA Modules:
  0.0 63.7 jit_solution(4041338653726391444)
XLA Ops:
  0.6 61.0 %shard_map.84 = (bf16[2,32,8192]{2,1,0:T(8,128)(2,1)}, bf16[2,32,1024]{2,1,0:T(8,128)(2,1)}) custom-call(bf16[32,8192]{1,0:T(8,128)(2,1)} %q_in.1, bf16[32,1024]{1,0:T(8,128)(2,1)} %k_in.1, bf16[32,1024]{1,0:T(8,128)(2,1)} %v_in.1, bf16[32,8192]{1,0:T(8,128)(2,1)} %g_in.1, s32[32]{0:T(128)} %lens.1), custom_call_target="tpu_custom_call" | custom-call | tf_op jit(solution)/shard_map/pallas_call | solution.py:281
  61.6 2.1 %shard_map.85 = (bf16[32,8192]{1,0:T(8,128)(2,1)}, bf16[32,8192]{1,0:T(8,128)(2,1)}, bf16[32,1024]{1,0:T(8,128)(2,1)}, bf16[32,1024]{1,0:T(8,128)(2,1)}) custom-call(bf16[2,32,8192]{2,1,0:T(8,128)(2,1)} %get-tuple-element.6.odq, bf16[2,32,1024]{2,1,0:T(8,128)(2,1)} %get-tuple-element.7.dkv), custom_call_target="tpu_custom_call" | custom-call | tf_op jit(solution)/shard_map/pallas_call | solution.py:317

commit v3 on v2

--- a/solution.py
+++ b/solution.py
@@ -118,6 +118,9 @@
     def rows_of(h):
         return pl.ds(pl.multiple_of(WINDOW - SHARD + h * PIECE, PIECE), PIECE)
 
+    def far_rows(h):
+        return pl.ds(pl.multiple_of(2 * SHARD + h * PIECE, PIECE), PIECE)
+
     def back(distance):
         return pl.ds(pl.multiple_of((4 - distance) * SHARD, SHARD), SHARD)
 
@@ -142,7 +145,8 @@
     local(g_in.at[:, columns(me, COLS)], qg.at[me, 1], qg_sem.at[0])
 
     barrier = pltpu.get_barrier_semaphore()
-    partners = [(c, peers[i]) for i in range(1, GROUPS)] + [other, ahead, behind]
+    partners = [(c, peers[i]) for i in range(1, GROUPS)] + [other]
+    partners += [(near, h) for near in (ahead[0], behind[0]) for h in peers]
     for partner in partners:
         pl.semaphore_signal(barrier, inc=1, device_id=partner, device_id_type=MESH)
     acc[...] = jnp.zeros_like(acc)
@@ -150,22 +154,32 @@
     landed(qg_own, stage_sem.at[1])
     pl.semaphore_wait(barrier, len(partners))
 
-    for i in range(1, GROUPS):
-        cols = columns(takers[i], HEAD_WIDTH)
-        send(kv_own.at[:, :, cols], kv.at[:, rows_of(me)], send_sem.at[0], kv_sem, (c, takers[i]))
-    for i in range(1, GROUPS):
+    for i in range(GROUPS):
+        piece = kv_own.at[:, :, columns(takers[i], HEAD_WIDTH)]
+        if i > 0:
+            send(piece, kv.at[:, rows_of(me)], send_sem.at[0], kv_sem, (c, takers[i]))
+    for i in range(GROUPS):
+        piece = kv_own.at[:, :, columns(takers[i], HEAD_WIDTH)]
+        send(piece, kv.at[:, far_rows(me)], send_sem.at[2], fwd_sem.at[0], (ahead[0], takers[i]))
+
+
+    def give(i):
         cols = columns(takers[i], COLS)
         send(qg_own.at[:, :, cols], qg.at[me], send_sem.at[1], qg_sem.at[i], (c, takers[i]))
 
+    for i in range(1, 4):
+        give(i)
+
+    landed(kv.at[:, back(2)], fwd_sem.at[0])
+    for n in range(2):
+        send(kv.at[n, back(2)], kv.at[n, back(4)], send_sem.at[3], fwd_sem.at[2 + n], ahead)
     landed(kv.at[:, own], kv_sem)
     for n in range(2):
-        send(kv.at[n, own], kv.at[n, back(2)], send_sem.at[2], fwd_sem.at[n], ahead)
+        send(kv.at[n, back(2 * core)], kv.at[n, back(1)], send_sem.at[4], swap_sem.at[n], other)
+    for i in range(4, GROUPS):
+        give(i)
     for n in range(2):
         kv_t[n, :, own] = kv[n, own, :].T
-    for n in range(2):
-        landed(kv.at[n, back(2)], fwd_sem.at[n])
-        send(kv.at[n, back(2)], kv.at[n, back(4)], send_sem.at[3], fwd_sem.at[2 + n], ahead)
-        send(kv.at[n, back(2 * core)], kv.at[n, back(1)], send_sem.at[4], swap_sem.at[n], other)
     for n in range(2):
         kv_t[n, :, 512:768] = kv[n, 512:768, :].T
     for n in range(2):

time: 64.8 us -> 58.1 us (0.90)
  the two profiles are of different devices: /device:TPU:1 before, /device:TPU:4 now
where the time goes in v3:
time: 58.1 us; the launch traced here: 57.9 us
  Pallas kernels  57.2 us (98%)
  between operations  0.64 us (1%)
    pallas_call x1, Pallas kernels, shards(): pl.pallas_call(kernel, out_shape=[jax.ShapeDtypeStruct((2, *wide), BF16),...  55.1 us
    pallas_call x1, Pallas kernels, shards(): pl.pallas_call(write, out_shape=[jax.ShapeDtypeStruct(shape, BF16) for sh...  2.11 us

profile of v3, /device:TPU:4, one launch (start us, length us, event | category | flops | bytes accessed | tf_op | source)
XLA Modules:
  0.0 57.9 jit_solution(9627132122015216070)
XLA Ops:
  0.6 55.1 %shard_map.84 = (bf16[2,32,8192]{2,1,0:T(8,128)(2,1)}, bf16[2,32,1024]{2,1,0:T(8,128)(2,1)}) custom-call(bf16[32,8192]{1,0:T(8,128)(2,1)} %q_in.1, bf16[32,1024]{1,0:T(8,128)(2,1)} %k_in.1, bf16[32,1024]{1,0:T(8,128)(2,1)} %v_in.1, bf16[32,8192]{1,0:T(8,128)(2,1)} %g_in.1, s32[32]{0:T(128)} %lens.1), custom_call_target="tpu_custom_call" | custom-call | tf_op jit(solution)/shard_map/pallas_call | solution.py:295
  55.8 2.1 %shard_map.85 = (bf16[32,8192]{1,0:T(8,128)(2,1)}, bf16[32,8192]{1,0:T(8,128)(2,1)}, bf16[32,1024]{1,0:T(8,128)(2,1)}, bf16[32,1024]{1,0:T(8,128)(2,1)}) custom-call(bf16[2,32,8192]{2,1,0:T(8,128)(2,1)} %get-tuple-element.6.odq, bf16[2,32,1024]{2,1,0:T(8,128)(2,1)} %get-tuple-element.7.dkv), custom_call_target="tpu_custom_call" | custom-call | tf_op jit(solution)/shard_map/pallas_call | solution.py:331

commit v4 on v3

--- a/solution.py
+++ b/solution.py
@@ -167,7 +167,7 @@
         cols = columns(takers[i], COLS)
         send(qg_own.at[:, :, cols], qg.at[me], send_sem.at[1], qg_sem.at[i], (c, takers[i]))
 
-    for i in range(1, 4):
+    for i in range(1, 6):
         give(i)
 
     landed(kv.at[:, back(2)], fwd_sem.at[0])
@@ -176,7 +176,7 @@
     landed(kv.at[:, own], kv_sem)
     for n in range(2):
         send(kv.at[n, back(2 * core)], kv.at[n, back(1)], send_sem.at[4], swap_sem.at[n], other)
-    for i in range(4, GROUPS):
+    for i in range(6, GROUPS):
         give(i)
     for n in range(2):
         kv_t[n, :, own] = kv[n, own, :].T
@@ -202,19 +202,23 @@
             piece_scores(pair[n], c * SHARD, lens, qg, kv, s_buf.at[n], dp_buf.at[n]) for n in range(2)
         ]
         done = [piece_forward(pair[n], scored[n], kv_t, odq, s_buf.at[n], p_buf.at[n]) for n in range(2)]
+        def give_back(which):
+            mine = odq_out.at[which, :, columns(me, COLS)]
+
+            @pl.when(i == 0)
+            def _():
+                local(odq.at[pair[0], which], mine, odq_sem)
+
+            @pl.when(i > 0)
+            def _():
+                send(odq.at[pair[0], which], mine, send_sem.at[6], odq_sem, (c, pair[0]))
+
+            send(odq.at[pair[1], which], mine, send_sem.at[6], odq_sem, (c, pair[1]))
+
+        give_back(0)
         for n in range(2):
             piece_backward(pair[n], done[n], kv_t, odq, acc, s_buf.at[n], dp_buf.at[n], p_buf.at[n])
-        mine = odq_out.at[:, :, columns(me, COLS)]
-
-        @pl.when(i == 0)
-        def _():
-            local(odq.at[pair[0]], mine, odq_sem)
-
-        @pl.when(i > 0)
-        def _():
-            send(odq.at[pair[0]], mine, send_sem.at[6], odq_sem, (c, pair[0]))
-
-        send(odq.at[pair[1]], mine, send_sem.at[6], odq_sem, (c, pair[1]))
+        give_back(1)
         return carry
 
     lax.fori_loop(0, GROUPS // 2, step, 0)

time: 58.1 us -> 57.4 us (0.988)
  the two profiles are of different devices: /device:TPU:4 before, /device:TPU:1 now
where the time goes in v4:
time: 57.4 us; the launch traced here: 57.2 us
  Pallas kernels  56.6 us (99%)
  between operations  0.64 us (1%)
    pallas_call x1, Pallas kernels, shards(): pl.pallas_call(kernel, out_shape=[jax.ShapeDtypeStruct((2, *wide), BF16),...  54.5 us
    pallas_call x1, Pallas kernels, shards(): pl.pallas_call(write, out_shape=[jax.ShapeDtypeStruct(shape, BF16) for sh...  2.11 us

profile of v4, /device:TPU:1, one launch (start us, length us, event | category | flops | bytes accessed | tf_op | source)
XLA Modules:
  0.0 57.2 jit_solution(5211349111690468950)
XLA Ops:
  0.6 54.5 %shard_map.84 = (bf16[2,32,8192]{2,1,0:T(8,128)(2,1)}, bf16[2,32,1024]{2,1,0:T(8,128)(2,1)}) custom-call(bf16[32,8192]{1,0:T(8,128)(2,1)} %q_in.1, bf16[32,1024]{1,0:T(8,128)(2,1)} %k_in.1, bf16[32,1024]{1,0:T(8,128)(2,1)} %v_in.1, bf16[32,8192]{1,0:T(8,128)(2,1)} %g_in.1, s32[32]{0:T(128)} %lens.1), custom_call_target="tpu_custom_call" | custom-call | tf_op jit(solution)/shard_map/pallas_call | solution.py:299
  55.1 2.1 %shard_map.85 = (bf16[32,8192]{1,0:T(8,128)(2,1)}, bf16[32,8192]{1,0:T(8,128)(2,1)}, bf16[32,1024]{1,0:T(8,128)(2,1)}, bf16[32,1024]{1,0:T(8,128)(2,1)}) custom-call(bf16[2,32,8192]{2,1,0:T(8,128)(2,1)} %get-tuple-element.6.odq, bf16[2,32,1024]{2,1,0:T(8,128)(2,1)} %get-tuple-element.7.dkv), custom_call_target="tpu_custom_call" | custom-call | tf_op jit(solution)/shard_map/pallas_call | solution.py:335

commit v5 on v4

--- a/solution.py
+++ b/solution.py
@@ -247,14 +247,13 @@
         base = part(n, 0) + jnp.where(first_core, swap_in[0, n].astype(F32), 0.0)
         landed(far_in.at[0, n], far_sem.at[2 + n])
         last[n] = (base + far_in[0, n].astype(F32)).astype(BF16)
-
-    def piece_of(h):
-        return last.at[:, pl.ds(pl.multiple_of(h * PIECE, PIECE), PIECE)]
-
-    mine = dkv_out.at[:, :, columns(me, HEAD_WIDTH)]
-    for i in range(1, GROUPS):
-        send(piece_of(peers[i]), mine, send_sem.at[11], dkv_sem, (c, peers[i]))
-    local(piece_of(me), mine, dkv_sem)
+        mine = dkv_out.at[n, :, columns(me, HEAD_WIDTH)]
+        for i, h in enumerate(peers):
+            piece = last.at[n, pl.ds(pl.multiple_of(h * PIECE, PIECE), PIECE)]
+            if i > 0:
+                send(piece, mine, send_sem.at[11], dkv_sem, (c, h))
+            else:
+                local(piece, mine, dkv_sem)
 
     others = pl.ds(0, GROUPS - 1)
     landed(kv.at[:, pl.ds(0, (GROUPS - 1) * PIECE)], send_sem.at[0])

time: 57.4 us -> 57.5 us (level)
  no operation moved by 1% of the time
where the time goes in v5:
time: 57.5 us; the launch traced here: 57.3 us
  Pallas kernels  56.7 us (99%)
  between operations  0.64 us (1%)
    pallas_call x1, Pallas kernels, shards(): pl.pallas_call(kernel, out_shape=[jax.ShapeDtypeStruct((2, *wide), BF16),...  54.6 us
    pallas_call x1, Pallas kernels, shards(): pl.pallas_call(write, out_shape=[jax.ShapeDtypeStruct(shape, BF16) for sh...  2.11 us

profile of v5, /device:TPU:1, one launch (start us, length us, event | category | flops | bytes accessed | tf_op | source)
XLA Modules:
  0.0 57.3 jit_solution(218390340541903492)
XLA Ops:
  0.6 54.6 %shard_map.84 = (bf16[2,32,8192]{2,1,0:T(8,128)(2,1)}, bf16[2,32,1024]{2,1,0:T(8,128)(2,1)}) custom-call(bf16[32,8192]{1,0:T(8,128)(2,1)} %q_in.1, bf16[32,1024]{1,0:T(8,128)(2,1)} %k_in.1, bf16[32,1024]{1,0:T(8,128)(2,1)} %v_in.1, bf16[32,8192]{1,0:T(8,128)(2,1)} %g_in.1, s32[32]{0:T(128)} %lens.1), custom_call_target="tpu_custom_call" | custom-call | tf_op jit(solution)/shard_map/pallas_call | solution.py:298
  55.2 2.1 %shard_map.85 = (bf16[32,8192]{1,0:T(8,128)(2,1)}, bf16[32,8192]{1,0:T(8,128)(2,1)}, bf16[32,1024]{1,0:T(8,128)(2,1)}, bf16[32,1024]{1,0:T(8,128)(2,1)}) custom-call(bf16[2,32,8192]{2,1,0:T(8,128)(2,1)} %get-tuple-element.6.odq, bf16[2,32,1024]{2,1,0:T(8,128)(2,1)} %get-tuple-element.7.dkv), custom_call_target="tpu_custom_call" | custom-call | tf_op jit(solution)/shard_map/pallas_call | solution.py:334
